TPU v7x, 32 devices: a whole 2x2x4 slice. The times are simulated.
32 devices in a mesh: batch: 4 (over y, x), tm: 8 (over z, core).
Axes of the slice: x: 2, y: 2, z: 4, core: 2. Of those that a mesh axis runs over, the one named last changes fastest.
Arguments:
- clips_in: bfloat16 [16, 128, 32768], P('batch', None, 'tm'), may hold values from -6 to 6
- conv_weight: bfloat16 [64, 64, 4], replicated, may hold values from -0.375 to 0.375
- conv_bias: float32 [64], replicated, may hold values from -3 to 3
- dilated_weight: bfloat16 [64, 64, 3], replicated, may hold values from -0.4375 to 0.4375
- dilated_bias: float32 [64], replicated, may hold values from -3 to 3
- mix_weight: bfloat16 [64, 64], replicated, may hold values from -0.75 to 0.75
- mix_bias: float32 [64], replicated, may hold values from -3 to 3
- frame_counts: int32 [16], P('batch'), may hold values from 16384 to 65536, as said below
- rate_groups: int32 [16], P('batch'), may hold values from 0 to 1
- out_grad: bfloat16 [16, 64, 32768], P('batch', None, 'tm'), may hold values from -6 to 6
Outputs:
- layer_out: bfloat16 [16, 64, 32768], P('batch', None, 'tm')
- clips_grad: bfloat16 [16, 128, 32768], P('batch', None, 'tm')
- conv_weight_grad: float32 [64, 64, 4], replicated
- conv_bias_grad: float32 [64], replicated
- dilated_weight_grad: float32 [64, 64, 3], replicated
- dilated_bias_grad: float32 [64], replicated
- mix_weight_grad: float32 [64, 64], replicated
- mix_bias_grad: float32 [64], replicated
Inputs may be any that keep to these rules, and one draw needn't show every extreme that they name: `frame_counts`: in each aligned block of 4 clips one clip, chosen by the seed, has count 2 * 32768 and group 0 in even blocks, 1 in odd blocks.
All inputs are finite; a program needn't handle non-finite values.
Results may differ from a plain program's by a relative error of at most 0.0065.
Values may be sent and summed in bfloat16 or wider, within the bound.
A program may use at most 64 MiB of HBM per device.

v0:
```python
import jax
import jax.numpy as jnp
from jax import lax
from jax.sharding import PartitionSpec as P

DILATION = 27


def with_halo(block, sides, width):
    for axis, dim in sides:
        count = lax.axis_size(axis)
        forward = [(i, i + 1) for i in range(count - 1)]
        backward = [(target, source) for source, target in forward]
        low = lax.ppermute(
            lax.slice_in_dim(block, block.shape[dim] - width, None, axis=dim), axis, forward
        )
        high = lax.ppermute(lax.slice_in_dim(block, 0, width, axis=dim), axis, backward)
        block = jnp.concatenate([low, block, high], axis=dim)
    return block


def gelu_back(value, upstream):
    return jax.vjp(jax.nn.gelu, value)[1](upstream)[0]


def apply_w(weight, signal):
    return jnp.einsum("oi,bit->bot", weight, signal, preferred_element_type=jnp.float32)


def apply_wt(weight, signal):
    return jnp.einsum("oi,bot->bit", weight, signal, preferred_element_type=jnp.float32)


def outer_sum(left, right):
    return jnp.einsum("bot,bit->oi", left, right, preferred_element_type=jnp.float32)


def frame_mask(valid_len, first, count):
    index = first + jnp.arange(count, dtype=jnp.int32)
    inside = (index[None, :] >= 0) & (index[None, :] < valid_len[:, None])
    return inside.astype(jnp.float32)[:, None, :]


def neighbours(padded, count):
    return (padded[:, :, 0:count], padded[:, :, 1 : count + 1], padded[:, :, 2 : count + 2])


def strided_conv(conv_weight, w_here, conv_bias, before, here, after, channels):
    total = conv_bias[None, :, None] + apply_w(conv_weight[:, :, 0], before[:, channels:])
    total = total + apply_w(w_here, here)
    return total + apply_w(conv_weight[:, :, 3], after[:, :channels])


def dilate(mid_wide, dilated_weight, dilated_bias, count):
    taps = [mid_wide[:, :, tap * DILATION : tap * DILATION + count] for tap in range(3)]
    total = dilated_bias[None, :, None]
    for tap in range(3):
        total = total + apply_w(dilated_weight[:, :, tap], taps[tap])
    return (taps, total)


def back_dilate(pre_wide, dilated_weight, count):
    total = apply_wt(dilated_weight[:, :, 0], pre_wide[:, :, 2 * DILATION : 2 * DILATION + count])
    for tap in range(1, 3):
        start = (2 - tap) * DILATION
        total = total + apply_wt(dilated_weight[:, :, tap], pre_wide[:, :, start : start + count])
    return total


def body(
    clips_in,
    conv_weight,
    conv_bias,
    dilated_weight,
    dilated_bias,
    mix_weight,
    mix_bias,
    frame_counts,
    rate_groups,
    out_grad,
):
    frame_span = out_grad.shape[2]
    channels = conv_weight.shape[0]
    position = lax.axis_index("tm")
    base = position * frame_span
    valid_len = jnp.minimum(frame_counts // (1 + rate_groups), frame_span * lax.axis_size("tm"))
    out_mask = frame_mask(valid_len, base, frame_span)
    masked = clips_in * out_mask.astype(jnp.bfloat16)
    w_here = jnp.concatenate([conv_weight[:, :, 1], conv_weight[:, :, 2]], axis=1)
    padded = with_halo(masked, (("tm", 2),), 1)
    before, here, after = neighbours(padded, frame_span)
    first_out = (
        strided_conv(conv_weight, w_here, conv_bias, before, here, after, channels) * out_mask
    )
    mid_act = jax.nn.gelu(first_out).astype(jnp.bfloat16)
    mid_wide = with_halo(mid_act, (("tm", 2),), DILATION)
    mid_taps, dilated_pre = dilate(mid_wide, dilated_weight, dilated_bias, frame_span)
    gated = jax.nn.gelu(dilated_pre).astype(jnp.bfloat16)
    branch_grad = (out_grad.astype(jnp.float32) * out_mask).astype(jnp.bfloat16)
    pre_grad = gelu_back(dilated_pre, apply_wt(mix_weight, branch_grad)).astype(jnp.bfloat16)
    pre_wide = with_halo(pre_grad, (("tm", 2),), DILATION)
    mid_grad = back_dilate(pre_wide, dilated_weight, frame_span)
    first_grad = (branch_grad.astype(jnp.float32) + gelu_back(first_out, mid_grad)).astype(
        jnp.bfloat16
    )
    conv_out_grad = first_grad * out_mask.astype(jnp.bfloat16)
    conv_wide = with_halo(conv_out_grad, (("tm", 2),), 1)
    branch = apply_w(mix_weight, gated) + mix_bias[None, :, None]
    layer_out = ((first_out + branch) * out_mask).astype(jnp.bfloat16)
    mix_weight_grad = outer_sum(branch_grad, gated)
    mix_bias_grad = jnp.sum(branch_grad.astype(jnp.float32), axis=(0, 2))
    dilated_bias_grad = jnp.sum(pre_grad.astype(jnp.float32), axis=(0, 2))
    dilated_weight_grad = jnp.stack(
        [outer_sum(pre_grad, mid_taps[tap]) for tap in range(3)], axis=2
    )
    conv_bias_grad = jnp.sum(conv_out_grad.astype(jnp.float32), axis=(0, 2))
    grad_before = outer_sum(conv_out_grad, before[:, channels:])
    grad_here = outer_sum(conv_out_grad, here)
    grad_after = outer_sum(conv_out_grad, after[:, :channels])
    conv_weight_grad = jnp.stack(
        [grad_before, grad_here[:, :channels], grad_here[:, channels:], grad_after], axis=2
    )
    grad_prev, grad_now, grad_next = neighbours(conv_wide, frame_span)
    side_terms = jnp.concatenate(
        [apply_wt(conv_weight[:, :, 3], grad_prev), apply_wt(conv_weight[:, :, 0], grad_next)],
        axis=1,
    )
    input_grad = (apply_wt(w_here, grad_now) + side_terms) * out_mask
    clips_grad = input_grad.astype(jnp.bfloat16)
    totals = lax.psum(
        (
            conv_weight_grad,
            conv_bias_grad,
            dilated_weight_grad,
            dilated_bias_grad,
            mix_weight_grad,
            mix_bias_grad,
        ),
        ("batch", "tm"),
    )
    return (layer_out, clips_grad, totals[0], totals[1], totals[2], totals[3], totals[4], totals[5])


def solution(mesh):
    placed = (
        P("batch", None, "tm"),
        P(),
        P(),
        P(),
        P(),
        P(),
        P(),
        P("batch"),
        P("batch"),
        P("batch", None, "tm"),
    )
    return jax.shard_map(
        body,
        mesh=mesh,
        in_specs=placed,
        out_specs=(P("batch", None, "tm"), P("batch", None, "tm"), P(), P(), P(), P(), P(), P()),
        check_vma=False,
    )
```

profile of v0, /device:TPU:0, one launch (start us, length us, event | category | flops | bytes accessed | tf_op | source)
XLA Modules:
  0.0 329.0 jit_solution(1326699966855282908)
XLA Ops:
  7.2 0.0 copy-start
  7.2 0.0 all-reduce.4.cloned.1.call-start
  7.3 0.8 fusion.54
  8.1 0.1 and_convert_fusion
  8.2 0.0 copy-start.3
  8.2 2.5 broadcast_multiply_fusion
  10.7 0.1 fusion.70
  10.8 1.3 collective-permute-start.1
  12.1 3.0 collective-permute-start
  15.2 0.1 fusion.74
  15.3 0.0 copy-start.2
  15.3 0.0 copy-start.5
  15.3 0.8 fusion.53
  16.1 0.8 copy-done.2
  16.9 1.0 convert_reduce_fusion
  17.9 1.2 fusion.8
  19.1 0.0 copy-start.4
  19.1 2.5 multiply_convert_fusion.2
  21.6 0.0 copy-start.6
  21.6 0.1 fusion.73
  21.7 1.3 collective-permute-start.3
  23.0 5.3 %collective-permute-start.2 = (bf16[4,64,27]{2,1,0:T(8,128)(2,1)S(1)}, bf16[4,64,27]{2,1,0:T(8,128)(2,1)S(1)}, u32[]{:S(2)}, u32[]{:S(2)}) collective-permute-start(bf16[4,64,27]{2,1,0:T(8,128)(2,1)S(1)} %get-tuple-element.28), channel_id=1, source_target_pairs={{0,1},{1,2},{2,3},{3,4},{4,5},{5,6},{6,7},{8,9},{9,10},{10,11},{11... | collective-permute-start | bytes 41480 | tf_op jit(solution)/shard_map/ppermute | solution.py:14
  28.4 0.7 fusion.43
  29.1 1.1 fusion.5
  30.2 0.0 collective-permute-done.3
  30.2 1.1 fusion.4
  31.3 2.5 fusion.36
  33.8 4.2 %convert_reduce_fusion.1 = (f32[64]{0:T(128)}, bf16[4,64,4096]{2,1,0:T(8,128)(2,1)S(1)}) fusion(f32[4,64,4096]{2,1,0:T(8,128)S(1)} %fusion.4, bf16[64,64]{1,0:T(8,128)(2,1)S(1)} %copy-done, bf16[4,64,4096]{2,1,0:T(8,128)(2,1)S(1)} %copy-done.2, f32[4,4096]{1,0:T(4,128)S(1)} %get-tuple-element.35), kind=kOutput, calls=%fused_computation.43 | convolution fusion | flops 160432064 | bytes 8462592 | tf_op jit(solution)/shard_map/oi,bot->bit/dot_general | solution.py:31
  38.0 0.9 fusion.75
  38.9 0.0 copy-start.7
  38.9 0.1 fusion.72
  39.0 0.8 fusion.45
  39.8 1.3 collective-permute-start.4
  41.1 4.9 %collective-permute-start.5 = (bf16[4,64,27]{2,1,0:T(8,128)(2,1)S(1)}, bf16[4,64,27]{2,1,0:T(8,128)(2,1)S(1)}, u32[]{:S(2)}, u32[]{:S(2)}) collective-permute-start(bf16[4,64,27]{2,1,0:T(8,128)(2,1)S(1)} %get-tuple-element.26), channel_id=1, source_target_pairs={{0,1},{1,2},{2,3},{3,4},{4,5},{5,6},{6,7},{8,9},{9,10},{10,11},{11... | collective-permute-start | bytes 41480 | tf_op jit(solution)/shard_map/ppermute | solution.py:14
  46.1 3.2 fusion.12
  49.3 1.1 fusion.33
  50.4 1.1 fusion.34
  51.5 1.0 fusion.30
  52.5 5.7 %convert_reduce_fusion.2 = (f32[64]{0:T(128)}, bf16[4,64,4096]{2,1,0:T(8,128)(2,1)S(1)}) fusion(bf16[4,4096]{1,0:T(4,128)(2,1)S(1)} %get-tuple-element.36, f32[4,64,4096]{2,1,0:T(8,128)S(1)} %get-tuple-element.38, f32[4,4096,64]{1,2,0:T(8,128)S(1)} %fusion.30, f32[4,4096,64]{1,2,0:T(8,128)S(1)} %fusion.45, bf16[64,64,3]{1,0,2:T(8,128)(2,1)S(1)} %copy-done.4, ...), kind=kOutput, calls=%fused_computation.44 | convolution fusion | flops 169869248 | bytes 19054848 | tf_op jit(solution)/shard_map/oi,bot->bit/dot_general | solution.py:31
  58.2 1.6 convolution_bitcast_fusion.3
  59.8 0.1 fusion.71
  59.9 0.1 slice_bitcast_fusion.1
  60.0 1.0 fusion.37
  61.0 1.1 fusion.38
  62.1 0.7 pad_maximum_fusion.20
  62.8 0.0 all-reduce.4.cloned.1.call-update
  62.8 0.0 all-reduce.6.cloned.1.call-start
  62.8 1.3 collective-permute-start.7
  64.1 0.7 pad_maximum_fusion.21
  64.8 5.1 %collective-permute-start.6 = (bf16[4,64,1]{2,1,0:T(8,128)(2,1)S(1)}, bf16[4,64,1]{2,1,0:T(8,128)(2,1)S(1)}, u32[]{:S(2)}, u32[]{:S(2)}) collective-permute-start(bf16[4,64,1]{2,1,0:T(8,128)(2,1)S(1)} %get-tuple-element.23), channel_id=1, source_target_pairs={{0,1},{1,2},{2,3},{3,4},{4,5},{5,6},{6,7},{8,9},{9,10},{10,11},{11... | collective-permute-start | bytes 1544 | tf_op jit(solution)/shard_map/ppermute | solution.py:14
  69.9 0.0 all-reduce.6.cloned.1.call-update
  69.9 2.0 convolution_bitcast_fusion
  72.0 2.0 convolution_bitcast_fusion.1
  74.0 0.0 copy-start.1
  74.0 7.0 %fusion.1 = bf16[4,128,4096]{1,2,0:T(8,128)(2,1)} fusion(f32[4,64,4096]{1,2,0:T(8,128)S(1)} %convolution_bitcast_fusion, f32[4,64,4096]{1,2,0:T(8,128)S(1)} %convolution_bitcast_fusion.1, bf16[4,64,4096]{2,1,0:T(8,128)(2,1)S(1)} %get-tuple-element.40, f32[4,4096]{1,0:T(4,128)S(1)} %get-tuple-element.35, bf16[64,64]{1,0:T(8,128)(2,1)S(1)} %get-tuple-element.43, ...), kind=kOutput, calls=%fused_computation.2 | convolution fusion | flops 276856832 | bytes 14761984 | tf_op jit(solution)/shard_map/oi,bot->bit/dot_general | solution.py:31
  81.0 6.4 %copy.30 = bf16[4,128,4096]{2,1,0:T(8,128)(2,1)} copy(bf16[4,128,4096]{1,2,0:T(8,128)(2,1)} %fusion.1) | data formatting | bytes 8388608
  87.4 100.4 %all-reduce.4.cloned.1.call-done = f32[64,64,4]{1,0,2:T(8,128)} async-done(((f32[64,64,4]{1,0,2:T(8,128)}), f32[64,64,4]{1,0,2:T(8,128)}) %all-reduce.4.cloned.1.call-update) | async-done | bytes 65552 | tf_op jit(solution)/shard_map/psum | solution.py:130
  187.8 1.6 copy.31
  189.4 126.4 %all-reduce.6.cloned.1.call-done = (f32[64]{0:T(128)}, f32[64,64,3]{1,0,2:T(8,128)}, f32[64]{0:T(128)}, f32[64,64]{1,0:T(8,128)}, f32[64]{0:T(128)}) async-done(((f32[64]{0:T(128)}, f32[64,64,3]{1,0,2:T(8,128)}, f32[64]{0:T(128)}, f32[64,64]{1,0:T(8,128)}, f32[64]{0:T(128)}), (f32[64]{0:T(128)}, f32[64,64,3]{1,0,2:T(8,128)}, f32[64]{0:T(128)}, f32[64,64]{1,0:T(8,128)}, ...) | async-done | bytes 66320 | tf_op jit(solution)/shard_map/psum | solution.py:130
  315.8 1.1 copy.68
  317.0 1.5 copy.69
  318.5 1.1 copy.70
  319.6 1.4 copy.71
  321.0 1.2 copy.72
  (17 shorter events, 0.1 us)
Async XLA Ops:
  7.2 26.6 %copy-start = (bf16[64,64]{1,0:T(8,128)(2,1)S(1)}, bf16[64,64]{1,0:T(8,128)(2,1)}, u32[]{:S(2)}) copy-start(bf16[64,64]{1,0:T(8,128)(2,1)} %param.15) | copy-start | bytes 24580
  7.2 180.6 %all-reduce.4.cloned.1.call-start = ((), (), s32[]{:S(2)}) async-start(), calls=%async_computation | async-start | bytes 262144 | tf_op jit(solution)/shard_map/psum | solution.py:130
  8.2 7.0 %copy-start.3 = (bf16[64,64,4]{1,2,0:T(4,128)(2,1)S(1)}, bf16[64,64,4]{1,2,0:T(4,128)(2,1)}, u32[]{:S(2)}) copy-start(bf16[64,64,4]{1,2,0:T(4,128)(2,1)} %param.11) | copy-start | bytes 98308
  10.8 8.3 %collective-permute-start.1 = (bf16[4,128,1]{2,1,0:T(8,128)(2,1)S(1)}, bf16[4,128,1]{2,1,0:T(8,128)(2,1)S(1)}, u32[]{:S(2)}, u32[]{:S(2)}) collective-permute-start(bf16[4,128,1]{2,1,0:T(8,128)(2,1)S(1)} %get-tuple-element.21), channel_id=1, source_target_pairs={{1,0},{2,1},{3,2},{4,3},{5,4},{6,5},{7,6},{9,8},{10,9},{11,10},{12... | collective-permute-start | bytes 3080 | tf_op jit(solution)/shard_map/ppermute | solution.py:17
  12.1 5.8 %collective-permute-start = (bf16[4,128,1]{2,1,0:T(8,128)(2,1)S(1)}, bf16[4,128,1]{2,1,0:T(8,128)(2,1)S(1)}, u32[]{:S(2)}, u32[]{:S(2)}) collective-permute-start(bf16[4,128,1]{2,1,0:T(8,128)(2,1)S(1)} %get-tuple-element.22), channel_id=1, source_target_pairs={{0,1},{1,2},{2,3},{3,4},{4,5},{5,6},{6,7},{8,9},{9,10},{10,11},{11... | collective-permute-start | bytes 3080 | tf_op jit(solution)/shard_map/ppermute | solution.py:14
  15.3 1.6 copy-start.2
  15.3 2.6 copy-start.5
  19.1 9.3 %copy-start.4 = (bf16[64,64,3]{1,0,2:T(8,128)(2,1)S(1)}, bf16[64,64,3]{1,0,2:T(8,128)(2,1)}, u32[]{:S(2)}) copy-start(bf16[64,64,3]{1,0,2:T(8,128)(2,1)} %param.13) | copy-start | bytes 73732
  21.6 7.5 %copy-start.6 = (f32[64]{0:T(128)S(1)}, f32[64]{0:T(128)}, u32[]{:S(2)}) copy-start(f32[64]{0:T(128)} %param.14) | copy-start | bytes 772
  21.7 8.5 %collective-permute-start.3 = (bf16[4,64,27]{2,1,0:T(8,128)(2,1)S(1)}, bf16[4,64,27]{2,1,0:T(8,128)(2,1)S(1)}, u32[]{:S(2)}, u32[]{:S(2)}) collective-permute-start(bf16[4,64,27]{2,1,0:T(8,128)(2,1)S(1)} %get-tuple-element.27), channel_id=1, source_target_pairs={{1,0},{2,1},{3,2},{4,3},{5,4},{6,5},{7,6},{9,8},{10,9},{11,10},{12... | collective-permute-start | bytes 41480 | tf_op jit(solution)/shard_map/ppermute | solution.py:17
  23.0 6.1 %collective-permute-start.2 = (bf16[4,64,27]{2,1,0:T(8,128)(2,1)S(1)}, bf16[4,64,27]{2,1,0:T(8,128)(2,1)S(1)}, u32[]{:S(2)}, u32[]{:S(2)}) collective-permute-start(bf16[4,64,27]{2,1,0:T(8,128)(2,1)S(1)} %get-tuple-element.28), channel_id=1, source_target_pairs={{0,1},{1,2},{2,3},{3,4},{4,5},{5,6},{6,7},{8,9},{9,10},{10,11},{11... | collective-permute-start | bytes 41480 | tf_op jit(solution)/shard_map/ppermute | solution.py:14
  38.9 7.1 %copy-start.7 = (f32[64]{0:T(128)S(1)}, f32[64]{0:T(128)}, u32[]{:S(2)}) copy-start(f32[64]{0:T(128)} %param.16) | copy-start | bytes 772
  39.8 12.7 %collective-permute-start.4 = (bf16[4,64,27]{2,1,0:T(8,128)(2,1)S(1)}, bf16[4,64,27]{2,1,0:T(8,128)(2,1)S(1)}, u32[]{:S(2)}, u32[]{:S(2)}) collective-permute-start(bf16[4,64,27]{2,1,0:T(8,128)(2,1)S(1)} %get-tuple-element.25), channel_id=1, source_target_pairs={{1,0},{2,1},{3,2},{4,3},{5,4},{6,5},{7,6},{9,8},{10,9},{11,10},{12... | collective-permute-start | bytes 41480 | tf_op jit(solution)/shard_map/ppermute | solution.py:17
  41.1 10.4 %collective-permute-start.5 = (bf16[4,64,27]{2,1,0:T(8,128)(2,1)S(1)}, bf16[4,64,27]{2,1,0:T(8,128)(2,1)S(1)}, u32[]{:S(2)}, u32[]{:S(2)}) collective-permute-start(bf16[4,64,27]{2,1,0:T(8,128)(2,1)S(1)} %get-tuple-element.26), channel_id=1, source_target_pairs={{0,1},{1,2},{2,3},{3,4},{4,5},{5,6},{6,7},{8,9},{9,10},{10,11},{11... | collective-permute-start | bytes 41480 | tf_op jit(solution)/shard_map/ppermute | solution.py:14
  62.8 253.1 %all-reduce.6.cloned.1.call-start = ((), (), s32[]{:S(2)}) async-start(), calls=%async_computation.1 | async-start | bytes 265216 | tf_op jit(solution)/shard_map/psum | solution.py:130
  62.8 7.1 %collective-permute-start.7 = (bf16[4,64,1]{2,1,0:T(8,128)(2,1)S(1)}, bf16[4,64,1]{2,1,0:T(8,128)(2,1)S(1)}, u32[]{:S(2)}, u32[]{:S(2)}) collective-permute-start(bf16[4,64,1]{2,1,0:T(8,128)(2,1)S(1)} %get-tuple-element.24), channel_id=1, source_target_pairs={{1,0},{2,1},{3,2},{4,3},{5,4},{6,5},{7,6},{9,8},{10,9},{11,10},{12... | collective-permute-start | bytes 1544 | tf_op jit(solution)/shard_map/ppermute | solution.py:17
  64.8 7.2 %collective-permute-start.6 = (bf16[4,64,1]{2,1,0:T(8,128)(2,1)S(1)}, bf16[4,64,1]{2,1,0:T(8,128)(2,1)S(1)}, u32[]{:S(2)}, u32[]{:S(2)}) collective-permute-start(bf16[4,64,1]{2,1,0:T(8,128)(2,1)S(1)} %get-tuple-element.23), channel_id=1, source_target_pairs={{0,1},{1,2},{2,3},{3,4},{4,5},{5,6},{6,7},{8,9},{9,10},{10,11},{11... | collective-permute-start | bytes 1544 | tf_op jit(solution)/shard_map/ppermute | solution.py:14
  74.0 248.2 %copy-start.1 = (bf16[64,64]{1,0:T(8,128)(2,1)S(1)}, bf16[64,64]{1,0:T(8,128)(2,1)}, u32[]{:S(2)}) copy-start(bf16[64,64]{1,0:T(8,128)(2,1)} %param.15) | copy-start | bytes 24580
Sparse Core Ops, SparseCore 0:
  62.9 124.8 all-reduce.3
  194.7 121.1 all-reduce.5
where the time goes:
time: 331 us; the launch traced here: 329 us
  waiting for transfers between devices  227 us (69%)
  matrix products  42.6 us (13%)
  starting transfers between devices  23.7 us (7%)
  local copies, waits for them, and re-layouts  15.8 us (5%)
  between operations  14.4 us (4%)
  other arithmetic  5.78 us (2%)
    psum x2, waiting for transfers between devices, body(): lax.psum((conv_weight_grad, conv_bias_grad, dilated_weight_grad, dilated_...  227 us
    dot_general x7, matrix products, apply_wt(): jnp.einsum('oi,bot->bit', weight, signal, preferred_element_type=jnp.floa...  22.8 us
    ppermute x4, starting transfers between devices, with_halo(): lax.ppermute(lax.slice_in_dim(block, block.shape[dim] - width, None, axis...  18.4 us
    unnamed x23, local copies, waits for them, and re-layouts  15.2 us
    dot_general x7, matrix products, apply_w(): jnp.einsum('oi,bit->bot', weight, signal, preferred_element_type=jnp.floa...  10.5 us
    dot_general x7, matrix products, outer_sum(): jnp.einsum('bot,bit->oi', left, right, preferred_element_type=jnp.float32)  9.23 us
  transfers between devices with their start and end apart: 10, of which 2 were waited for; matrix products, arithmetic and copies ran while one was open for 9% of the time, Pallas kernels for 0%

commit v1 on v0

v1 whole, which is shorter than its diff:
```python
import functools

import jax
import jax.numpy as jnp
from jax import lax
from jax.experimental import pallas as pl
from jax.experimental.pallas import tpu as pltpu
from jax.sharding import PartitionSpec as P

DILATION = 27
EDGE = 128
CHUNK = 2048
PIECE = 32
MESH = pl.DeviceIdType.MESH
F32 = jnp.float32
BF16 = jnp.bfloat16
C0 = 0.7978845608028654
C1 = 0.044715


def dot(a, b):
    return lax.dot_general(a, b, (((1,), (0,)), ((), ())), preferred_element_type=F32)


def dot_t(a, b):
    return lax.dot_general(a, b, (((1,), (1,)), ((), ())), preferred_element_type=F32)


def gelu_parts(x):
    square = x * x
    s = 0.5 + 0.5 * jnp.tanh(x * (C0 + (C0 * C1) * square))
    value = x * s
    slope = s + (value - value * s) * (2 * C0 + (6 * C0 * C1) * square)
    return value, slope


def tall(rows, copies):
    return jnp.concatenate([rows] * copies, axis=0)


def wide(tile, count):
    return jnp.concatenate([tile] * count, axis=1)


def lane_groups(value):
    total = value[:, :EDGE]
    for start in range(EDGE, value.shape[1], EDGE):
        total = total + value[:, start : start + EDGE]
    return total


def compute(
    span,
    total,
    chunk,
    place,
    counts,
    groups,
    x_ref,
    xh_ref,
    og_ref,
    ogh_ref,
    wc,
    wd,
    wm,
    wdt,
    wct,
    biases,
    out_ref,
    clips_ref,
    sums_ref,
    pconv,
    pdil,
    pmix,
    psum,
    xs,
    bg,
    first,
    slope1,
    mid,
    midm,
    midp,
    x1m,
    x0p,
    pre,
    prem,
    prep,
    grad,
    gradm,
    gradp,
):
    ch = 64
    b = pl.program_id(0)
    off = 2 * EDGE
    base = place[0] * span
    valid = jnp.minimum(lax.shift_right_logical(counts[b], groups[b]), total)

    @pl.when(b == 0)
    def _():
        for ref in (xs, mid, midm, midp, x1m, x0p, pre, prem, prep, grad, gradm, gradp):
            for start in (0, span + 3 * EDGE):
                ref[:, start : start + EDGE] = jnp.zeros((ref.shape[0], EDGE), ref.dtype)
        for ref in (pconv, pdil, pmix, psum):
            ref[...] = jnp.zeros(ref.shape, ref.dtype)

    def mask_rows(t, n):
        frame = base + t + lax.broadcasted_iota(jnp.int32, (16, n), 1)
        return ((frame >= 0) & (frame < valid)).astype(F32)

    def put(ref, start, value):
        ref[:, start : start + value.shape[1]] = value

    def stage0(t, n):
        low = tall(mask_rows(t, n).astype(BF16), ch // 16)
        if t < 0:
            x, og = xh_ref[0, 0], ogh_ref[0, 0]
        elif t >= span:
            x, og = xh_ref[0, 1], ogh_ref[0, 1]
        else:
            x, og = x_ref[0, :, t : t + n], og_ref[0, :, t : t + n]
        dst = slice(t + off, t + off + n)
        even = x[:ch] * low
        odd = x[ch:] * low
        xs[:ch, dst] = even
        xs[ch:, dst] = odd
        put(x1m, t + off + 1, odd)
        put(x0p, t + off - 1, even)
        bg[:, dst] = og * low

    def stage1(t, n):
        here = slice(t + off, t + off + n)
        taps = jnp.concatenate([x1m[:, here], xs[:, here], x0p[:, here]], axis=0)
        mask = tall(mask_rows(t, n), ch // 16)
        f = (dot(wc[...], taps) + wide(biases[0], n // EDGE)) * mask
        value, slope = gelu_parts(f)
        first[:, here] = f
        slope1[:, here] = slope
        low = value.astype(BF16)
        mid[:, here] = low
        put(midm, t + off + DILATION, low)
        put(midp, t + off - DILATION, low)

    def stage2(t, n):
        here = slice(t + off, t + off + n)
        inner = 0 <= t < span
        taps = jnp.concatenate([midm[:, here], mid[:, here], midp[:, here]], axis=0)
        dilated = dot(wd[...], taps) + wide(biases[1], n // EDGE)
        value, slope = gelu_parts(dilated)
        branch_grad = bg[:, here]
        if inner:
            gated = value.astype(BF16)
            both = dot(wm[...], jnp.concatenate([gated, branch_grad], axis=0))
            mask = tall(mask_rows(t, n), ch // 16)
            layer = (first[:, here] + both[:ch] + wide(biases[2], n // EDGE)) * mask
            out_ref[0, :, t : t + n] = layer.astype(BF16)
            up = both[ch:]
            pmix[...] += dot_t(branch_grad, gated)
            psum[2] += lane_groups(branch_grad.astype(F32))
        else:
            up = dot(wm[ch:, ch:], branch_grad)
        pg = (up * slope).astype(BF16)
        pre[:, here] = pg
        put(prem, t + off + DILATION, pg)
        put(prep, t + off - DILATION, pg)
        if inner:
            psum[1] += lane_groups(pg.astype(F32))

    def stage3(t, n):
        here = slice(t + off, t + off + n)
        before = prem[:, here]
        now = pre[:, here]
        taps = jnp.concatenate([prep[:, here], now, before], axis=0)
        mid_grad = dot(wdt[...], taps)
        mask = tall(mask_rows(t, n), ch // 16)
        g = ((bg[:, here].astype(F32) + mid_grad * slope1[:, here]) * mask).astype(BF16)
        grad[:, here] = g
        put(gradm, t + off + 1, g)
        put(gradp, t + off - 1, g)
        if 0 <= t < span:
            pdil[...] += dot_t(
                jnp.concatenate([now, before], axis=0),
                jnp.concatenate([mid[:, here], midm[:, here]], axis=0),
            )
            psum[0] += lane_groups(g.astype(F32))

    def stage4(t, n):
        here = slice(t + off, t + off + n)
        g = grad[:, here]
        before = gradm[:, here]
        y = jnp.concatenate([x1m[:, here], xs[:ch, here]], axis=0)
        if t < span:
            after = gradp[:, here]
            low = tall(mask_rows(t, n), 2 * ch // 16)
            dx = dot(wct[...], jnp.concatenate([before, g, after], axis=0)) * low
            clips_ref[0, :, t : t + n] = dx.astype(BF16)
        if t == 0:
            lane = lax.broadcasted_iota(jnp.int32, (16, n), 1)
            own = tall((lane > 0).astype(F32).astype(BF16), ch // 16)
            before = before * own
        pconv[...] += dot_t(jnp.concatenate([g, before], axis=0), y)

    def stage4_edge():
        t, n = span, EDGE
        here = slice(t + off, t + off + n)
        before = gradm[:, here]
        lane = lax.broadcasted_iota(jnp.int32, (16, n), 1)
        own = tall((lane == 0).astype(F32).astype(BF16), ch // 16)
        y = jnp.concatenate([x1m[:, here], xs[:ch, here]], axis=0)
        pconv[ch:, :] += dot_t(before * own, y)

    inner = [(t, chunk) for t in range(0, span, chunk)]
    pieces = [(-EDGE, EDGE)] + inner + [(span, EDGE)]
    count = len(pieces)
    for step in range(count + 6):
        if 0 <= step - 6 < count and 0 <= pieces[step - 6][0] < span:
            stage4(*pieces[step - 6])
        if 0 <= step - 4 < count:
            stage3(*pieces[step - 4])
        if 0 <= step - 2 < count:
            stage2(*pieces[step - 2])
        if step == 0:
            stage0(*pieces[0])
        if step + 1 < count:
            stage0(*pieces[step + 1])
        if step < count:
            stage1(*pieces[step])
    stage4_edge()

    @pl.when(b == pl.num_programs(0) - 1)
    def _():
        rows = [pconv[...], pdil[:ch, :], jnp.concatenate([pdil[ch:, :ch], pmix[...]], axis=1)]
        at = 0
        for block in rows:
            sums_ref[at : at + block.shape[0], :] = block.astype(BF16)
            at += block.shape[0]
        lines = [jnp.sum(psum[k].T, axis=0, keepdims=True) for k in range(3)]
        lines = jnp.concatenate(lines + [jnp.zeros((13, ch), F32)], axis=0)
        lines = jnp.concatenate([lines, jnp.zeros_like(lines)], axis=1)
        sums_ref[at : at + 16, :] = lines.astype(BF16)
        sums_ref[at + 16 :, :] = jnp.zeros((sums_ref.shape[0] - at - 16, 2 * ch), BF16)


def compute_call(span, total, clips, chunk, rows=288):
    ch = 64
    lanes = span + 4 * EDGE
    whole = lambda shape: pl.BlockSpec(shape, lambda b: (0,) * len(shape))
    smem = pl.BlockSpec(memory_space=pltpu.SMEM)
    clip = lambda *shape: pl.BlockSpec((1, *shape), lambda b: (b,) + (0,) * len(shape))
    sums = [(2 * ch, 2 * ch), (2 * ch, 2 * ch), (ch, ch), (3, ch, EDGE)]
    return pl.pallas_call(
        functools.partial(compute, span, total, chunk),
        name="layer",
        grid=(clips,),
        in_specs=[smem, smem, smem, clip(2 * ch, span), clip(2, 2 * ch, EDGE), clip(ch, span), clip(2, ch, EDGE)]
        + [whole(s) for s in ((ch, 4 * ch), (ch, 3 * ch), (2 * ch, 2 * ch), (ch, 3 * ch), (2 * ch, 3 * ch), (3, ch, EDGE))],
        out_specs=[clip(ch, span), clip(2 * ch, span), whole((rows, 2 * ch))],
        out_shape=[
            jax.ShapeDtypeStruct((clips, ch, span), BF16),
            jax.ShapeDtypeStruct((clips, 2 * ch, span), BF16),
            jax.ShapeDtypeStruct((rows, 2 * ch), BF16),
        ],
        scratch_shapes=[pltpu.VMEM(s, F32) for s in sums]
        + [pltpu.VMEM((2 * ch, lanes), BF16)]
        + [pltpu.VMEM((ch, lanes), BF16)]
        + [pltpu.VMEM((ch, lanes), F32)] * 2
        + [pltpu.VMEM((ch, lanes), BF16)] * 11,
        compiler_params=pltpu.CompilerParams(vmem_limit_bytes=63 << 20),
    )


def edges(
    parts,
    x_ref,
    og_ref,
    cw,
    dw,
    mw,
    cb,
    db,
    mb,
    xh_ref,
    ogh_ref,
    wc,
    wd,
    wm,
    wdt,
    wct,
    biases,
    xzero,
    ogzero,
    send,
    recv,
    fill,
):
    ch = 64
    span = x_ref.shape[2]
    row, place = lax.axis_index("batch"), lax.axis_index("tm")
    has = (place > 0, place < parts - 1)
    other = (place - 1, place + 1)
    barrier = pltpu.get_barrier_semaphore()
    for side in range(2):
        @pl.when(has[side])
        def _():
            pl.semaphore_signal(barrier, inc=1, device_id=(row, other[side]), device_id_type=MESH)
    xzero[...] = jnp.zeros(xzero.shape, BF16)
    ogzero[...] = jnp.zeros(ogzero.shape, BF16)
    peers = jnp.where(has[0], 1, 0) + jnp.where(has[1], 1, 0)
    pl.semaphore_wait(barrier, peers)

    def moves(side):
        cut = pl.ds(0, EDGE) if side == 0 else pl.ds(span - EDGE, EDGE)
        return [
            pltpu.make_async_remote_copy(
                src_ref=src.at[:, :, cut],
                dst_ref=dst.at[:, 1 - side],
                send_sem=send.at[side, k],
                recv_sem=recv.at[1 - side, k],
                device_id=(row, other[side]),
                device_id_type=MESH,
            )
            for k, (src, dst) in enumerate(((x_ref, xh_ref), (og_ref, ogh_ref)))
        ]

    def blanks(side):
        return [
            pltpu.make_async_copy(zero, dst.at[:, side], fill.at[side, k])
            for k, (zero, dst) in enumerate(((xzero, xh_ref), (ogzero, ogh_ref)))
        ]

    for side in range(2):
        @pl.when(has[side])
        def _():
            for move in moves(side):
                move.start()

        @pl.when(jnp.logical_not(has[side]))
        def _():
            for blank in blanks(side):
                blank.start()

    taps = [cw[:, k, :] for k in range(4)]
    flip = lambda w: w.astype(F32).T.astype(BF16)
    zero = jnp.zeros((ch, ch), BF16)
    for k in range(4):
        wc[:, k * ch : (k + 1) * ch] = taps[k]
    for k in range(3):
        wd[:, k * ch : (k + 1) * ch] = dw[k]
        wdt[:, k * ch : (k + 1) * ch] = flip(dw[k])
    wm[...] = jnp.concatenate(
        [jnp.concatenate([mw[...], zero], axis=1), jnp.concatenate([zero, flip(mw[...])], axis=1)], axis=0
    )
    back = [flip(tap) for tap in taps]
    wct[:ch, :] = jnp.concatenate([back[3], back[1], zero], axis=1)
    wct[ch:, :] = jnp.concatenate([zero, back[2], back[0]], axis=1)
    for k, line in enumerate((cb, db, mb)):
        biases[k] = jnp.broadcast_to(line[...], (EDGE, ch)).T

    for side in range(2):
        @pl.when(has[side])
        def _():
            for move in moves(side):
                move.wait_send()
            for move in moves(1 - side):
                move.wait_recv()

        @pl.when(jnp.logical_not(has[side]))
        def _():
            for blank in blanks(side):
                blank.wait()


def edges_call(clips, span, parts):
    ch = 64
    vmem = pl.BlockSpec(memory_space=pltpu.VMEM)
    hbm = pl.BlockSpec(memory_space=pl.ANY)
    shapes = [(ch, 4 * ch), (ch, 3 * ch), (2 * ch, 2 * ch), (ch, 3 * ch), (2 * ch, 3 * ch)]
    return pl.pallas_call(
        functools.partial(edges, parts),
        name="edges",
        in_specs=[hbm, hbm] + [vmem] * 6,
        out_specs=[hbm, hbm] + [vmem] * 6,
        out_shape=[
            jax.ShapeDtypeStruct((clips, 2, 2 * ch, EDGE), BF16),
            jax.ShapeDtypeStruct((clips, 2, ch, EDGE), BF16),
        ]
        + [jax.ShapeDtypeStruct(s, BF16) for s in shapes]
        + [jax.ShapeDtypeStruct((3, ch, EDGE), F32)],
        scratch_shapes=[
            pltpu.VMEM((clips, 2 * ch, EDGE), BF16),
            pltpu.VMEM((clips, ch, EDGE), BF16),
            pltpu.SemaphoreType.DMA((2, 2)),
            pltpu.SemaphoreType.DMA((2, 2)),
            pltpu.SemaphoreType.DMA((2, 2)),
        ],
        compiler_params=pltpu.CompilerParams(collective_id=0, has_side_effects=True, vmem_limit_bytes=63 << 20),
    )


def owner_list(rows, parts, pieces):
    half = parts // 2
    order = sorted(range(half), key=lambda q: abs(2 * q - half + 1))
    spots = [(r, 2 * q + 1) for q in order for r in range(rows)]
    spots += [(r, 2 * q) for q in order for r in range(rows)]
    return spots[:pieces]


def total_kernel(rows, parts, owners, x, out, slots, send, recv, send2, recv2):
    count = rows * parts
    pieces = len(owners)
    row, place = lax.axis_index("batch"), lax.axis_index("tm")
    me = row * parts + place
    barrier = pltpu.get_barrier_semaphore()

    def others(action):
        def step(r, carry):
            target = lax.rem(me + r, count)
            action(target // parts, lax.rem(target, parts))
            return carry

        lax.fori_loop(1, count, step, 0)

    others(lambda r, p: pl.semaphore_signal(barrier, inc=1, device_id=(r, p), device_id_type=MESH))
    pl.semaphore_wait(barrier, count - 1)
    for piece, (r, p) in enumerate(owners):
        home = r * parts + p

        @pl.when(me != home)
        def _():
            pltpu.make_async_remote_copy(
                src_ref=x.at[piece],
                dst_ref=slots.at[lax.rem(me - home + count, count) - 1],
                send_sem=send,
                recv_sem=recv,
                device_id=(r, p),
                device_id_type=MESH,
            ).start()

    for piece, (r, p) in enumerate(owners):
        @pl.when(me == r * parts + p)
        def _():
            pltpu.make_async_copy(slots, slots, recv).wait()
            total = x[piece].astype(F32)
            for k in range(count - 1):
                total = total + slots[k].astype(F32)
            out[piece] = total.astype(BF16)
            others(
                lambda tr, tp: pltpu.make_async_remote_copy(
                    src_ref=out.at[piece],
                    dst_ref=out.at[piece],
                    send_sem=send2,
                    recv_sem=recv2,
                    device_id=(tr, tp),
                    device_id_type=MESH,
                ).start()
            )

    owner = functools.reduce(jnp.logical_or, [me == r * parts + p for r, p in owners])

    @pl.when(owner)
    def _():
        rest = out.at[pl.ds(0, pieces - 1)]
        pltpu.make_async_copy(rest, rest, recv2).wait()
        sent = x.at[pl.ds(0, pieces - 1)]
        pltpu.make_async_copy(sent, sent, send).wait()
        pltpu.make_async_copy(slots, slots, send2).wait()

    @pl.when(jnp.logical_not(owner))
    def _():
        pltpu.make_async_copy(out, out, recv2).wait()
        pltpu.make_async_copy(x, x, send).wait()


def total_call(rows, parts, pieces):
    shape = (pieces, PIECE, 128)
    vmem = pl.BlockSpec(memory_space=pltpu.VMEM)
    return pl.pallas_call(
        functools.partial(total_kernel, rows, parts, owner_list(rows, parts, pieces)),
        name="total",
        in_specs=[vmem],
        out_specs=vmem,
        out_shape=jax.ShapeDtypeStruct(shape, BF16),
        scratch_shapes=[pltpu.VMEM((rows * parts - 1, PIECE, 128), BF16)] + [pltpu.SemaphoreType.DMA] * 4,
        compiler_params=pltpu.CompilerParams(collective_id=1, has_side_effects=True, vmem_limit_bytes=63 << 20),
    )


def unpack(sums, cg, cb, dg, db, mg, mb):
    ch = 64
    at = lambda start, count: sums[start : start + count, :].astype(F32)
    low, high = at(0, ch), at(ch, ch)
    for k, block in enumerate((low[:, :ch], low[:, ch:], high[:, :ch], high[:, ch:])):
        cg[:, k, :] = block
    block = at(2 * ch, ch)
    dg[1] = block[:, :ch]
    dg[0] = block[:, ch:]
    block = at(3 * ch, ch)
    dg[2] = block[:, :ch]
    mg[...] = block[:, ch:]
    lines = at(4 * ch, 16)[:, :ch]
    for k, ref in enumerate((cb, db, mb)):
        ref[...] = lines[k : k + 1]


def unpack_call():
    ch = 64
    vmem = pl.BlockSpec(memory_space=pltpu.VMEM)
    shapes = [(ch, 4, ch), (1, ch), (3, ch, ch), (1, ch), (ch, ch), (1, ch)]
    return pl.pallas_call(
        unpack,
        name="unpack",
        in_specs=[vmem],
        out_specs=[vmem] * 6,
        out_shape=[jax.ShapeDtypeStruct(s, F32) for s in shapes],
    )


def body(rows, parts, clips_in, cw, cb, dw, db, mw, mb, counts, groups, out_grad):
    clips, ch, span = out_grad.shape
    pieces = -(-(4 * ch + 16) // PIECE)
    place = lax.axis_index("tm").astype(jnp.int32)[None]
    xh, ogh, *params = edges_call(clips, span, parts)(
        clips_in, out_grad, cw.transpose(0, 2, 1), dw.transpose(2, 0, 1), mw, cb[None], db[None], mb[None]
    )
    layer_out, clips_grad, sums = compute_call(span, span * parts, clips, CHUNK, pieces * PIECE)(
        place, counts, groups, clips_in, xh, out_grad, ogh, *params
    )
    sums = total_call(rows, parts, pieces)(sums.reshape(pieces, PIECE, 2 * ch))
    cg, cbg, dg, dbg, mg, mbg = unpack_call()(sums.reshape(pieces * PIECE, 2 * ch))
    return (layer_out, clips_grad, cg.transpose(0, 2, 1), cbg[0], dg.transpose(1, 2, 0), dbg[0], mg, mbg[0])


def solution(mesh):
    split = P("batch", None, "tm")
    placed = (split, P(), P(), P(), P(), P(), P(), P("batch"), P("batch"), split)
    return jax.shard_map(
        functools.partial(body, mesh.shape["batch"], mesh.shape["tm"]),
        mesh=mesh,
        in_specs=placed,
        out_specs=(split, split) + (P(),) * 6,
        check_vma=False,
    )
```

time: 331 us -> 44.8 us (0.14)
  waiting for transfers between devices: 227 us -> 0 us
  Pallas kernels: 0 us -> 43.9 us
  matrix products: 42.6 us -> 0 us
  starting transfers between devices: 23.7 us -> 0 us
  local copies, waits for them, and re-layouts: 15.8 us -> 0 us
  between operations: 14.4 us -> 0.66 us
  other arithmetic: 5.78 us -> 0 us
    psum x2 -> x0, waiting for transfers between devices: 227 us -> none  [body(): lax.psum((conv_weight_grad, conv_bias_grad, dilated_weight_grad, dilated_...]
    pallas_call x0 -> x4, Pallas kernels: none -> 43.9 us  [the longest x1 18.5 us: body(): compute_call(span, span * parts, clips, CHUNK, pieces * PIECE)]
    dot_general x21 -> x0, matrix products: 42.6 us -> none  [the longest x7 22.8 us: apply_wt(): jnp.einsum('oi,bot->bit', weight, signal, preferred_element_type=jnp.floa...]
    ppermute x8 -> x0, starting transfers between devices: 23.6 us -> none  [the longest x4 18.4 us: with_halo(): lax.ppermute(lax.slice_in_dim(block, block.shape[dim] - width, None, axis...]
    unnamed x23 -> x0, local copies, waits for them, and re-layouts: 15.2 us -> none
  transfers between devices with their start and end apart: 10 -> 0, of which waited for: 2 -> 0; matrix products, arithmetic and copies ran while one was open for 9% -> 0% of each run, Pallas kernels for 0% -> 0%
where the time goes in v1:
time: 44.8 us; the launch traced here: 44.6 us
  Pallas kernels  43.9 us (98%)
  between operations  0.66 us (1%)
    pallas_call x1, Pallas kernels, body(): compute_call(span, span * parts, clips, CHUNK, pieces * PIECE)  18.5 us
    pallas_call x1, Pallas kernels, body(): sums = total_call(rows, parts, pieces)(sums.reshape(pieces, PIECE, 2 * ch))  17.5 us
    pallas_call x1, Pallas kernels, body(): edges_call(clips, span, parts)  6.15 us
    pallas_call x1, Pallas kernels, body(): unpack_call()(sums.reshape(pieces * PIECE, 2 * ch))  1.79 us

profile of v1, /device:TPU:0, one launch (start us, length us, event | category | flops | bytes accessed | tf_op | source)
XLA Modules:
  0.0 44.6 jit_solution(16982022739903744169)
XLA Ops:
  0.6 6.2 %edges.1 = (bf16[4,2,128,128]{3,2,1,0:T(8,128)(2,1)}, bf16[4,2,64,128]{3,2,1,0:T(8,128)(2,1)}, bf16[64,256]{1,0:T(8,128)(2,1)}, bf16[64,192]{1,0:T(8,128)(2,1)},...) custom-call(bf16[4,128,4096]{2,1,0:T(8,128)(2,1)} %x_ref.3, ...), custom_call_target="tpu_custom_call" | custom-call | tf_op jit(solution)/shard_map/edges/pallas_call | solution.py:521
  6.8 18.5 %layer.1 = (bf16[4,64,4096]{2,1,0:T(8,128)(2,1)}, bf16[4,128,4096]{2,1,0:T(8,128)(2,1)}, bf16[288,128]{1,0:T(8,128)(2,1)}) custom-call(s32[1]{0:T(128)} %bitcast.place, s32[4]{0:T(128)} %counts.1, s32[4]{0:T(128)} %groups.1, bf16[4,128,4096]{2,1,0:T(8,128)(2,1)} %x_ref.3, bf16[4,2,128,128]{3,2,1,0:T(8,128)(2,1)} %get-tuple-element.25.xh_ref, ...), custom_call_target="tpu_custom_call" | custom-call | tf_op jit(solution)/shard_map/layer/pallas_call | solution.py:524
  25.3 17.5 %total.1 = bf16[9,32,128]{2,1,0:T(8,128)(2,1)} custom-call(bf16[9,32,128]{2,1,0:T(8,128)(2,1)} %bitcast.14), custom_call_target="tpu_custom_call" | custom-call | tf_op jit(solution)/shard_map/total/pallas_call | solution.py:527
  42.8 1.8 %unpack.1 = (f32[64,4,64]{2,1,0:T(4,128)}, f32[1,64]{1,0:T(1,128)}, f32[3,64,64]{2,1,0:T(8,128)}, f32[1,64]{1,0:T(1,128)}, f32[64,64]{1,0:T(8,128)}, /*index=5*/f32[1,64]{1,0:T(1,128)}) custom-call(bf16[288,128]{1,0:T(8,128)(2,1)} %bitcast.13), custom_call_target="tpu_custom_call" | custom-call | tf_op jit(solution)/shard_map/unpack/pallas_call | solution.py:528

commit v2 on v0

v2 whole, which is shorter than its diff:
```python
import functools

import jax
import jax.numpy as jnp
from jax import lax
from jax.experimental import pallas as pl
from jax.experimental.pallas import tpu as pltpu
from jax.sharding import PartitionSpec as P

DILATION = 27
EDGE = 128
OFF = 2 * EDGE
CHUNK = 2048
PIECE = 32
MESH = pl.DeviceIdType.MESH
F32 = jnp.float32
BF16 = jnp.bfloat16
C0 = 0.7978845608028654
C1 = 0.044715


def dot(a, b):
    return lax.dot_general(a, b, (((1,), (0,)), ((), ())), preferred_element_type=F32)


def dot_t(a, b):
    return lax.dot_general(a, b, (((1,), (1,)), ((), ())), preferred_element_type=F32)


def stack(*rows):
    return jnp.concatenate(rows, axis=0)


def beside(*parts):
    return jnp.concatenate(parts, axis=1)


def gelu_parts(half):
    square = half * half
    t = jnp.tanh(half * (2 * C0 + (8 * C0 * C1) * square))
    up = 1.0 + t
    value = half * up
    return value, up + (value * (1.0 - t)) * (2 * C0 + (24 * C0 * C1) * square)


def tall(rows, copies):
    return jnp.concatenate([rows] * copies, axis=0)


def wide(tile, count):
    return jnp.concatenate([tile] * count, axis=1)


def lane_groups(value):
    total = value[:, :EDGE]
    for start in range(EDGE, value.shape[1], EDGE):
        total = total + value[:, start : start + EDGE]
    return total


def owner_list(rows, parts, pieces):
    half = parts // 2
    order = sorted(range(half), key=lambda q: abs(2 * q - half + 1))
    spots = [(r, 2 * q + 1) for q in order for r in range(rows)]
    spots += [(r, 2 * q) for q in order for r in range(rows)]
    return spots[:pieces]


def layer(
    rows,
    parts,
    owners,
    counts,
    groups,
    x_ref,
    og_ref,
    cw,
    dw,
    mw,
    cb,
    db,
    mb,
    outs,
    dxs,
    total_ref,
    wc,
    wd,
    wm,
    wu,
    wdt,
    wct,
    biases,
    x0,
    x1,
    bg,
    x0p,
    x1m,
    half,
    slope,
    mid,
    midm,
    midp,
    gated,
    pre,
    prem,
    prep,
    grad,
    gradm,
    gradp,
    xh,
    ogh,
    pconv,
    pdil,
    pmix,
    psum,
    parcel,
    slots,
    in_sem,
    send,
    recv,
    send1,
    recv1,
    send2,
    recv2,
):
    ch = 64
    clips, _, span = og_ref.shape
    chunk = min(CHUNK, span)
    pieces = len(owners)
    count = rows * parts
    row, place = lax.axis_index("batch"), lax.axis_index("tm")
    me = row * parts + place
    base = place * span

    def others(action):
        def step(r, carry):
            target = lax.rem(me + r, count)
            action(target // parts, lax.rem(target, parts))
            return carry

        lax.fori_loop(1, count, step, 0)

    inside = pl.ds(OFF, span)

    def fetches(b):
        return [
            pltpu.make_async_copy(x_ref.at[b, pl.ds(0, ch)], x0.at[b, :, inside], in_sem.at[b, 0]),
            pltpu.make_async_copy(x_ref.at[b, pl.ds(ch, ch)], x1.at[b, :, inside], in_sem.at[b, 1]),
            pltpu.make_async_copy(og_ref.at[b], bg.at[b, :, inside], in_sem.at[b, 2]),
        ]

    for b in range(clips):
        for fetch in fetches(b):
            fetch.start()
    xh[...] = jnp.zeros(xh.shape, BF16)
    ogh[...] = jnp.zeros(ogh.shape, BF16)
    barrier = pltpu.get_barrier_semaphore()
    others(lambda r, p: pl.semaphore_signal(barrier, inc=1, device_id=(r, p), device_id_type=MESH))

    flip = lambda w: w.astype(F32).T.astype(BF16)
    taps = [cw[:, k, :] for k in range(4)]
    zero = jnp.zeros((ch, ch), BF16)
    for k in range(4):
        wc[:, k * ch : (k + 1) * ch] = taps[k] * 0.5
    for k in range(3):
        wd[:, k * ch : (k + 1) * ch] = dw[k] * 0.5
        wdt[:, k * ch : (k + 1) * ch] = flip(dw[k]) * 0.5
    wm[...] = mw[...] * 0.5
    wu[...] = flip(mw[...]) * 0.5
    back = [flip(tap) for tap in taps]
    wct[:ch, :] = beside(back[3], back[1], zero)
    wct[ch:, :] = beside(zero, back[2], back[0])
    for k, line in enumerate((cb, db, mb)):
        biases[k] = jnp.broadcast_to(line[...] * 0.5, (EDGE, ch)).T

    left, right = pl.ds(OFF - EDGE, EDGE), pl.ds(OFF + span, EDGE)
    for ref in (gradm,):
        ref[:, :, OFF : OFF + EDGE] = jnp.zeros((clips, ch, EDGE), BF16)
    for ref in (x0, x1, mid, grad, gradm):
        ref[:, :, 0:EDGE] = jnp.zeros((clips, ch, EDGE), BF16)
        ref[:, :, OFF + span : OFF + span + EDGE] = jnp.zeros((clips, ch, EDGE), BF16)
        ref[:, :, OFF + span + EDGE :] = jnp.zeros((clips, ch, EDGE), BF16)
    for ref in (x0p, x1m, midm, midp, prem, prep):
        for at in (0, OFF + span, OFF + span + EDGE):
            ref[:, :, at : at + EDGE] = jnp.zeros((clips, ch, EDGE), BF16)
    for ref in (pconv, pdil, pmix, psum):
        ref[...] = jnp.zeros(ref.shape, F32)

    def masks(b, t, n, high=1.0):
        valid = jnp.minimum(lax.shift_right_logical(counts[b], groups[b]), span * parts)
        frame = base + t + lax.broadcasted_iota(jnp.int32, (16, n), 1)
        return jnp.where((frame >= 0) & (frame < valid), high, 0.0)

    def put(ref, b, start, value):
        ref[b, :, start : start + value.shape[1]] = value

    has = (place > 0, place < parts - 1)
    other = (place - 1, place + 1)

    def moves(side):
        cut = pl.ds(0, EDGE) if side == 0 else pl.ds(span - EDGE, EDGE)
        return [
            pltpu.make_async_remote_copy(
                src_ref=src.at[:, :, cut],
                dst_ref=dst.at[1 - side],
                send_sem=send.at[side, k],
                recv_sem=recv.at[1 - side, k],
                device_id=(row, other[side]),
                device_id_type=MESH,
            )
            for k, (src, dst) in enumerate(((x_ref, xh), (og_ref, ogh)))
        ]

    def stage1(b, t, n):
        here = slice(t + OFF, t + OFF + n)
        taps = stack(x1m[b, :, here], x0[b, :, here], x1[b, :, here], x0p[b, :, here])
        h = dot(wc[...], taps) + wide(biases[0], n // EDGE)
        value, s = gelu_parts(h)
        half[b, :, here] = h
        slope[b, :, here] = s
        return value

    def shifted(refs, b, t, step, low):
        now, before, after = refs
        now[b, :, t + OFF : t + OFF + low.shape[1]] = low
        put(before, b, t + OFF + step, low)
        put(after, b, t + OFF - step, low)

    def first(b, carry):
        for fetch in fetches(b):
            fetch.wait()
        for t in range(0, span, chunk):
            here = slice(t + OFF, t + OFF + chunk)
            low = tall(masks(b, t, chunk).astype(BF16), ch // 16)
            even = x0[b, :, here] * low
            x0[b, :, here] = even
            put(x0p, b, t + OFF - 1, even)
            put(x1m, b, t + OFF + 1, x1[b, :, here])
            bg[b, :, here] = bg[b, :, here] * low
        for t in range(0, span, chunk):
            start, n = max(t, EDGE), min(t + chunk, span - EDGE) - max(t, EDGE)
            low = tall(masks(b, start, n).astype(BF16), ch // 16)
            shifted((mid, midm, midp), b, start, DILATION, stage1(b, start, n).astype(BF16) * low)

        @pl.when(b == 0)
        def _():
            pl.semaphore_wait(barrier, count - 1)
            for side in range(2):
                @pl.when(has[side])
                def _():
                    for move in moves(side):
                        move.start()

        return carry

    lax.fori_loop(0, clips, first, 0)

    for side in range(2):
        @pl.when(has[side])
        def _():
            for move in moves(1 - side):
                move.wait_recv()

    sides = ((0, -EDGE), (1, span))

    def outside(b, carry):
        lows = [tall(masks(b, t, EDGE).astype(BF16), ch // 16) for _, t in sides]
        for (side, t), low in zip(sides, lows):
            here = slice(t + OFF, t + OFF + EDGE)
            even = xh[side, b, :ch] * low
            odd = xh[side, b, ch:]
            x0[b, :, here] = even
            x1[b, :, here] = odd
            put(x0p, b, t + OFF - 1, even)
            put(x1m, b, t + OFF + 1, odd)
            bg[b, :, here] = ogh[side, b] * low
        starts = (-EDGE, span - EDGE)
        spots = [slice(t + OFF, t + OFF + 2 * EDGE) for t in starts]
        both = lambda ref: beside(*[ref[b, :, spot] for spot in spots])
        h = dot(wc[...], stack(both(x1m), both(x0), both(x1), both(x0p))) + wide(biases[0], 4)
        value, s = gelu_parts(h)
        for k, t in enumerate(starts):
            cut = slice(2 * k * EDGE, 2 * (k + 1) * EDGE)
            half[b, :, spots[k]] = h[:, cut]
            slope[b, :, spots[k]] = s[:, cut]
            low = tall(masks(b, t, 2 * EDGE).astype(BF16), ch // 16)
            shifted((mid, midm, midp), b, t, DILATION, value[:, cut].astype(BF16) * low)
        spots = [slice(t + OFF, t + OFF + EDGE) for _, t in sides]
        d = dot(wd[...], stack(both(midm), both(mid), both(midp))) + wide(biases[1], 2)
        _, s = gelu_parts(d)
        low = (dot(wu[...], both(bg)) * s).astype(BF16)
        for k, (side, t) in enumerate(sides):
            shifted((pre, prem, prep), b, t, DILATION, low[:, k * EDGE : (k + 1) * EDGE])
        return carry

    lax.fori_loop(0, clips, outside, 0)

    ones = jnp.ones((16, chunk), BF16)

    def second(b, carry):
        for t in range(0, span, chunk):
            here = slice(t + OFF, t + OFF + chunk)
            d = dot(wd[...], stack(midm[b, :, here], mid[b, :, here], midp[b, :, here]))
            d = d + wide(biases[1], chunk // EDGE)
            value, s = gelu_parts(d)
            low = value.astype(BF16)
            gated[b, :, t : t + chunk] = low
            pg = dot(wu[...], bg[b, :, here]) * s
            psum[1] += lane_groups(pg)
            shifted((pre, prem, prep), b, t, DILATION, pg.astype(BF16))
            pmix[:, : ch + 16] += dot_t(bg[b, :, here], stack(low, ones))
        for t in range(0, span, chunk):
            here = slice(t + OFF, t + OFF + chunk)
            mask = tall(masks(b, t, chunk), ch // 16)
            mid_grad = dot(wdt[...], stack(prep[b, :, here], pre[b, :, here], prem[b, :, here]))
            g = (bg[b, :, here].astype(F32) + mid_grad * slope[b, :, here]) * mask
            psum[0] += lane_groups(g)
            shifted((grad, gradm, gradp), b, t, 1, g.astype(BF16))
            pdil[...] += dot_t(
                stack(pre[b, :, here], prem[b, :, here]), stack(mid[b, :, here], midm[b, :, here])
            )
        wide_here = slice(OFF, OFF + span + EDGE)
        pconv[...] += dot_t(
            stack(grad[b, :, wide_here], gradm[b, :, wide_here]), stack(x1m[b, :, wide_here], x0[b, :, wide_here])
        )
        return carry

    lax.fori_loop(0, clips, second, 0)

    at = 0
    flat = [
        pconv[...],
        pdil[:ch, :],
        beside(pdil[ch:, :ch], pmix[:, :ch]),
    ]
    lines = [jnp.sum(psum[k].T, axis=0, keepdims=True) for k in range(2)]
    lines.append(pmix[:, ch:].T[:1, :])
    lines = stack(*lines, jnp.zeros((PIECE - 3, ch), F32))
    flat.append(beside(lines, jnp.zeros_like(lines)))
    for block in flat:
        for start in range(0, block.shape[0], PIECE):
            parcel[at] = block[start : start + PIECE, :].astype(BF16)
            at += 1
    for piece, (r, p) in enumerate(owners):
        home = r * parts + p

        @pl.when(me != home)
        def _():
            pltpu.make_async_remote_copy(
                src_ref=parcel.at[piece],
                dst_ref=slots.at[lax.rem(me - home + count, count) - 1],
                send_sem=send1,
                recv_sem=recv1,
                device_id=(r, p),
                device_id_type=MESH,
            ).start()

    def third(b, carry):
        for k, (side, t) in enumerate(sides):
            here = slice(t + OFF, t + OFF + EDGE)
            mask = tall(masks(b, t, EDGE), ch // 16)
            mid_grad = dot(wdt[...], stack(prep[b, :, here], pre[b, :, here], prem[b, :, here]))
            g = (bg[b, :, here].astype(F32) + mid_grad * slope[b, :, here]) * mask
            low = g.astype(BF16)
            if side == 0:
                put(gradm, b, t + OFF + 1, low)
            else:
                put(gradp, b, t + OFF - 1, low)
        for t in range(0, span, chunk):
            here = slice(t + OFF, t + OFF + chunk)
            there = slice(t, t + chunk)
            mask = masks(b, t, chunk, 2.0).astype(BF16)
            total = half[b, :, here] + dot(wm[...], gated[b, :, there]) + wide(biases[2], chunk // EDGE)
            outs[b, :, there] = total.astype(BF16) * tall(mask, ch // 16)
            low = masks(b, t, chunk).astype(BF16)
            dx = dot(wct[...], stack(gradm[b, :, here], grad[b, :, here], gradp[b, :, here]))
            dxs[b, :, there] = dx.astype(BF16) * tall(low, 2 * ch // 16)
        return carry

    lax.fori_loop(0, clips, third, 0)

    for piece, (r, p) in enumerate(owners):
        @pl.when(me == r * parts + p)
        def _():
            pltpu.make_async_copy(slots, slots, recv1).wait()
            total = parcel[piece].astype(F32)
            for k in range(count - 1):
                total = total + slots[k].astype(F32)
            total_ref[piece] = total.astype(BF16)
            others(
                lambda tr, tp: pltpu.make_async_remote_copy(
                    src_ref=total_ref.at[piece],
                    dst_ref=total_ref.at[piece],
                    send_sem=send2,
                    recv_sem=recv2,
                    device_id=(tr, tp),
                    device_id_type=MESH,
                ).start()
            )

    for side in range(2):
        @pl.when(has[side])
        def _():
            for move in moves(side):
                move.wait_send()
    owner = functools.reduce(jnp.logical_or, [me == r * parts + p for r, p in owners])

    @pl.when(owner)
    def _():
        rest = total_ref.at[pl.ds(0, pieces - 1)]
        pltpu.make_async_copy(rest, rest, recv2).wait()
        sent = parcel.at[pl.ds(0, pieces - 1)]
        pltpu.make_async_copy(sent, sent, send1).wait()
        pltpu.make_async_copy(slots, slots, send2).wait()

    @pl.when(jnp.logical_not(owner))
    def _():
        pltpu.make_async_copy(total_ref, total_ref, recv2).wait()
        pltpu.make_async_copy(parcel, parcel, send1).wait()


def layer_call(rows, parts, clips, span, pieces):
    ch = 64
    lanes = span + 4 * EDGE
    smem = pl.BlockSpec(memory_space=pltpu.SMEM)
    vmem = pl.BlockSpec(memory_space=pltpu.VMEM)
    hbm = pl.BlockSpec(memory_space=pl.ANY)
    low = pltpu.VMEM((clips, ch, lanes), BF16)
    high = pltpu.VMEM((clips, ch, lanes), F32)
    dma = pltpu.SemaphoreType.DMA
    return pl.pallas_call(
        functools.partial(layer, rows, parts, owner_list(rows, parts, pieces)),
        name="layer",
        in_specs=[smem, smem, hbm, hbm] + [vmem] * 6,
        out_specs=[vmem, vmem, vmem],
        out_shape=[
            pltpu.VMEM((clips, ch, span), BF16),
            pltpu.VMEM((clips, 2 * ch, span), BF16),
            pltpu.VMEM((pieces, PIECE, 2 * ch), BF16),
        ],
        scratch_shapes=[
            pltpu.VMEM((ch, 4 * ch), BF16),
            pltpu.VMEM((ch, 3 * ch), BF16),
            pltpu.VMEM((ch, ch), BF16),
            pltpu.VMEM((ch, ch), BF16),
            pltpu.VMEM((ch, 3 * ch), BF16),
            pltpu.VMEM((2 * ch, 3 * ch), BF16),
            pltpu.VMEM((3, ch, EDGE), F32),
        ]
        + [low] * 5
        + [high] * 2
        + [low] * 3
        + [pltpu.VMEM((clips, ch, span), BF16)]
        + [low] * 6
        + [
            pltpu.VMEM((2, clips, 2 * ch, EDGE), BF16),
            pltpu.VMEM((2, clips, ch, EDGE), BF16),
            pltpu.VMEM((2 * ch, 2 * ch), F32),
            pltpu.VMEM((2 * ch, 2 * ch), F32),
            pltpu.VMEM((ch, 2 * ch), F32),
            pltpu.VMEM((2, ch, EDGE), F32),
            pltpu.VMEM((pieces, PIECE, 2 * ch), BF16),
            pltpu.VMEM((rows * parts - 1, PIECE, 2 * ch), BF16),
            dma((clips, 3)),
            dma((2, 2)),
            dma((2, 2)),
            dma,
            dma,
            dma,
            dma,
        ],
        compiler_params=pltpu.CompilerParams(collective_id=0, has_side_effects=True, vmem_limit_bytes=54 << 20),
    )


def hand_over(out_in, clips_in, sums, out, clips, cg, cb, dg, db, mg, mb, sem):
    ch = 64
    moves = []
    for b in range(out.shape[0]):
        for k, (src, dst) in enumerate(((out_in, out), (clips_in, clips))):
            moves.append(pltpu.make_async_copy(src.at[b], dst.at[b], sem.at[b, k]))
    for move in moves:
        move.start()
    at = lambda start, count: sums[start : start + count, :].astype(F32)
    low, high = at(0, ch), at(ch, ch)
    for k, block in enumerate((low[:, :ch], low[:, ch:], high[:, :ch], high[:, ch:])):
        cg[:, k, :] = block
    block = at(2 * ch, ch)
    dg[1] = block[:, :ch]
    dg[0] = block[:, ch:]
    block = at(3 * ch, ch)
    dg[2] = block[:, :ch]
    mg[...] = block[:, ch:]
    lines = at(4 * ch, 16)[:, :ch]
    for k, ref in enumerate((cb, db, mb)):
        ref[...] = lines[k : k + 1]
    for move in moves:
        move.wait()


def hand_over_call(out, clips):
    ch = 64
    vmem = pl.BlockSpec(memory_space=pltpu.VMEM)
    hbm = pl.BlockSpec(memory_space=pl.ANY)
    shapes = [(ch, 4, ch), (1, ch), (3, ch, ch), (1, ch), (ch, ch), (1, ch)]
    like = lambda a: jax.ShapeDtypeStruct(a.shape, a.dtype)
    return pl.pallas_call(
        hand_over,
        name="hand_over",
        in_specs=[vmem, vmem, vmem],
        out_specs=[hbm, hbm] + [vmem] * 6,
        out_shape=[like(out), like(clips)] + [jax.ShapeDtypeStruct(s, F32) for s in shapes],
        scratch_shapes=[pltpu.SemaphoreType.DMA((out.shape[0], 2))],
        compiler_params=pltpu.CompilerParams(vmem_limit_bytes=8 << 20),
    )


def body(rows, parts, clips_in, cw, cb, dw, db, mw, mb, counts, groups, out_grad):
    clips, ch, span = out_grad.shape
    pieces = -(-(4 * ch + 16) // PIECE)
    layer_out, clips_grad, sums = layer_call(rows, parts, clips, span, pieces)(
        counts, groups, clips_in, out_grad, cw.transpose(0, 2, 1), dw.transpose(2, 0, 1), mw, cb[None], db[None], mb[None]
    )
    layer_out, clips_grad, cg, cbg, dg, dbg, mg, mbg = hand_over_call(layer_out, clips_grad)(
        layer_out, clips_grad, sums.reshape(pieces * PIECE, 2 * ch)
    )
    return (layer_out, clips_grad, cg.transpose(0, 2, 1), cbg[0], dg.transpose(1, 2, 0), dbg[0], mg, mbg[0])


def solution(mesh):
    split = P("batch", None, "tm")
    placed = (split, P(), P(), P(), P(), P(), P(), P("batch"), P("batch"), split)
    return jax.shard_map(
        functools.partial(body, mesh.shape["batch"], mesh.shape["tm"]),
        mesh=mesh,
        in_specs=placed,
        out_specs=(split, split) + (P(),) * 6,
        check_vma=False,
    )
```

time: 331 us -> 35.3 us (0.11)
  waiting for transfers between devices: 227 us -> 0 us
  matrix products: 42.6 us -> 0 us
  Pallas kernels: 0 us -> 34.5 us
  starting transfers between devices: 23.7 us -> 0 us
  local copies, waits for them, and re-layouts: 15.8 us -> 0 us
  between operations: 14.4 us -> 0.64 us
  other arithmetic: 5.78 us -> 0 us
    psum x2 -> x0, waiting for transfers between devices: 227 us -> none  [body(): lax.psum((conv_weight_grad, conv_bias_grad, dilated_weight_grad, dilated_...]
    dot_general x21 -> x0, matrix products: 42.6 us -> none  [the longest x7 22.8 us: apply_wt(): jnp.einsum('oi,bot->bit', weight, signal, preferred_element_type=jnp.floa...]
    pallas_call x0 -> x2, Pallas kernels: none -> 34.5 us  [the longest x1 31 us: body(): layer_call(rows, parts, clips, span, pieces)]
    ppermute x8 -> x0, starting transfers between devices: 23.6 us -> none  [the longest x4 18.4 us: with_halo(): lax.ppermute(lax.slice_in_dim(block, block.shape[dim] - width, None, axis...]
    unnamed x23 -> x0, local copies, waits for them, and re-layouts: 15.2 us -> none
  transfers between devices with their start and end apart: 10 -> 0, of which waited for: 2 -> 0; matrix products, arithmetic and copies ran while one was open for 9% -> 0% of each run, Pallas kernels for 0% -> 0%
where the time goes in v2:
time: 35.3 us; the launch traced here: 35.1 us
  Pallas kernels  34.5 us (98%)
  between operations  0.64 us (2%)
    pallas_call x1, Pallas kernels, body(): layer_call(rows, parts, clips, span, pieces)  31 us
    pallas_call x1, Pallas kernels, body(): hand_over_call(layer_out, clips_grad)  3.45 us

profile of v2, /device:TPU:0, one launch (start us, length us, event | category | flops | bytes accessed | tf_op | source)
XLA Modules:
  0.0 35.1 jit_solution(7106571624481437799)
XLA Ops:
  0.6 31.0 %layer.1 = (bf16[4,64,4096]{2,1,0:T(8,128)(2,1)S(1)}, bf16[4,128,4096]{2,1,0:T(8,128)(2,1)S(1)}, bf16[9,32,128]{2,1,0:T(8,128)(2,1)S(1)}) custom-call(s32[4]{0:T(128)} %counts.1, s32[4]{0:T(128)} %groups.1, bf16[4,128,4096]{2,1,0:T(8,128)(2,1)} %x_ref.1, bf16[4,64,4096]{2,1,0:T(8,128)(2,1)} %og_ref.1, bf16[64,4,64]{2,1,0:T(4,128)(2,1)} %bitcast.12, ...), custom_call_target="tpu_custom_call" | custom-call | tf_op jit(solution)/shard_map/layer/pallas_call | solution.py:521
  31.7 3.5 %hand_over.1 = (bf16[4,64,4096]{2,1,0:T(8,128)(2,1)}, bf16[4,128,4096]{2,1,0:T(8,128)(2,1)}, f32[64,4,64]{2,1,0:T(4,128)}, f32[1,64]{1,0:T(1,128)}, f32[3,64,64]...) custom-call(bf16[4,64,4096]{2,1,0:T(8,128)(2,1)S(1)} %get-tuple-element.19.out_in, ...), custom_call_target="tpu_custom_call" | custom-call | tf_op jit(solution)/shard_map/hand_over/pallas_call | solution.py:524

commit v3 on v2

--- a/solution.py
+++ b/solution.py
@@ -86,7 +86,6 @@
     wc,
     wd,
     wm,
-    wu,
     wdt,
     wct,
     biases,
@@ -163,26 +162,20 @@
     for k in range(4):
         wc[:, k * ch : (k + 1) * ch] = taps[k] * 0.5
     for k in range(3):
-        wd[:, k * ch : (k + 1) * ch] = dw[k] * 0.5
+        wd[:ch, k * ch : (k + 1) * ch] = dw[k] * 0.5
+        wd[ch:, k * ch : (k + 1) * ch] = zero
         wdt[:, k * ch : (k + 1) * ch] = flip(dw[k]) * 0.5
     wm[...] = mw[...] * 0.5
-    wu[...] = flip(mw[...]) * 0.5
+    wd[:ch, 3 * ch :] = zero
+    wd[ch:, 3 * ch :] = flip(mw[...]) * 0.5
     back = [flip(tap) for tap in taps]
     wct[:ch, :] = beside(back[3], back[1], zero)
     wct[ch:, :] = beside(zero, back[2], back[0])
     for k, line in enumerate((cb, db, mb)):
         biases[k] = jnp.broadcast_to(line[...] * 0.5, (EDGE, ch)).T
 
-    left, right = pl.ds(OFF - EDGE, EDGE), pl.ds(OFF + span, EDGE)
-    for ref in (gradm,):
-        ref[:, :, OFF : OFF + EDGE] = jnp.zeros((clips, ch, EDGE), BF16)
-    for ref in (x0, x1, mid, grad, gradm):
-        ref[:, :, 0:EDGE] = jnp.zeros((clips, ch, EDGE), BF16)
-        ref[:, :, OFF + span : OFF + span + EDGE] = jnp.zeros((clips, ch, EDGE), BF16)
-        ref[:, :, OFF + span + EDGE :] = jnp.zeros((clips, ch, EDGE), BF16)
-    for ref in (x0p, x1m, midm, midp, prem, prep):
-        for at in (0, OFF + span, OFF + span + EDGE):
-            ref[:, :, at : at + EDGE] = jnp.zeros((clips, ch, EDGE), BF16)
+    for ref, at in ((gradm, OFF), (gradm, OFF + span), (grad, OFF + span)):
+        ref[:, :, at : at + EDGE] = jnp.zeros((clips, ch, EDGE), BF16)
     for ref in (pconv, pdil, pmix, psum):
         ref[...] = jnp.zeros(ref.shape, F32)
 
@@ -211,49 +204,137 @@
             for k, (src, dst) in enumerate(((x_ref, xh), (og_ref, ogh)))
         ]
 
-    def stage1(b, t, n):
-        here = slice(t + OFF, t + OFF + n)
-        taps = stack(x1m[b, :, here], x0[b, :, here], x1[b, :, here], x0p[b, :, here])
-        h = dot(wc[...], taps) + wide(biases[0], n // EDGE)
+    def spot(t, n):
+        return slice(t + OFF, t + OFF + n)
+
+    def gather(ref, where):
+        return beside(*[ref[b, :, spot(t, n)] for b, t, n in where])
+
+    def cuts(where):
+        at = 0
+        for b, t, n in where:
+            yield b, t, n, slice(at, at + n)
+            at += n
+
+    def spread(refs, where, step, low):
+        now, before, after = refs
+        for b, t, n, cut in cuts(where):
+            now[b, :, spot(t, n)] = low[:, cut]
+            put(before, b, t + OFF + step, low[:, cut])
+            put(after, b, t + OFF - step, low[:, cut])
+
+    def lows(where):
+        return beside(*[tall(masks(b, t, n).astype(BF16), ch // 16) for b, t, n in where])
+
+    def stage0(b, t, n):
+        here = spot(t, n)
+        low = lows([(b, t, n)])
+        even = x0[b, :, here] * low
+        x0[b, :, here] = even
+        put(x0p, b, t + OFF - 1, even)
+        put(x1m, b, t + OFF + 1, x1[b, :, here])
+        bg[b, :, here] = bg[b, :, here] * low
+
+    def stage1(where):
+        taps = stack(gather(x1m, where), gather(x0, where), gather(x1, where), gather(x0p, where))
+        h = dot(wc[...], taps)
+        h = h + wide(biases[0], h.shape[1] // EDGE)
         value, s = gelu_parts(h)
-        half[b, :, here] = h
-        slope[b, :, here] = s
-        return value
-
-    def shifted(refs, b, t, step, low):
-        now, before, after = refs
-        now[b, :, t + OFF : t + OFF + low.shape[1]] = low
-        put(before, b, t + OFF + step, low)
-        put(after, b, t + OFF - step, low)
-
-    def first(b, carry):
-        for fetch in fetches(b):
-            fetch.wait()
-        for t in range(0, span, chunk):
-            here = slice(t + OFF, t + OFF + chunk)
-            low = tall(masks(b, t, chunk).astype(BF16), ch // 16)
-            even = x0[b, :, here] * low
-            x0[b, :, here] = even
-            put(x0p, b, t + OFF - 1, even)
-            put(x1m, b, t + OFF + 1, x1[b, :, here])
-            bg[b, :, here] = bg[b, :, here] * low
-        for t in range(0, span, chunk):
-            start, n = max(t, EDGE), min(t + chunk, span - EDGE) - max(t, EDGE)
-            low = tall(masks(b, start, n).astype(BF16), ch // 16)
-            shifted((mid, midm, midp), b, start, DILATION, stage1(b, start, n).astype(BF16) * low)
-
-        @pl.when(b == 0)
+        for b, t, n, cut in cuts(where):
+            half[b, :, spot(t, n)] = h[:, cut]
+            slope[b, :, spot(t, n)] = s[:, cut]
+        spread((mid, midm, midp), where, DILATION, value.astype(BF16) * lows(where))
+
+    def own(where):
+        kept = [(b, max(t, 0), min(t + n, span) - max(t, 0)) for b, t, n in where]
+        return kept, [
+            slice(cut.start + kt - t, cut.start + kt - t + kn)
+            for (b, t, n, cut), (_, kt, kn) in zip(cuts(where), kept)
+        ]
+
+    def stage2(where):
+        taps = stack(gather(midm, where), gather(mid, where), gather(midp, where), gather(bg, where))
+        both = dot(wd[...], taps)
+        d = both[:ch] + wide(biases[1], both.shape[1] // EDGE)
+        value, s = gelu_parts(d)
+        pg = both[ch:] * s
+        spread((pre, prem, prep), where, DILATION, pg.astype(BF16))
+        kept, inner = own(where)
+        low = value.astype(BF16)
+        for (b, t, n), cut in zip(kept, inner):
+            gated[b, :, t : t + n] = low[:, cut]
+            psum[1] += lane_groups(pg[:, cut])
+        low = beside(*[low[:, cut] for cut in inner])
+        ones = jnp.ones((16, low.shape[1]), BF16)
+        pmix[:, : ch + 16] += dot_t(gather(bg, kept), stack(low, ones))
+
+    def stage3(where, halo=False):
+        mid_grad = dot(wdt[...], stack(gather(prep, where), gather(pre, where), gather(prem, where)))
+        mask = beside(*[tall(masks(b, t, n), ch // 16) for b, t, n in where])
+        g = (gather(bg, where).astype(F32) + mid_grad * gather(slope, where)) * mask
+        low = g.astype(BF16)
+        kept, inner = own(where)
+        for (b, t, n), cut in zip(kept, inner):
+            psum[0] += lane_groups(g[:, cut])
+            spread((grad, gradm, gradp), [(b, t, n)], 1, low[:, cut])
+        return low
+
+    def dilated_sums(where):
+        pdil[...] += dot_t(
+            stack(gather(pre, where), gather(prem, where)), stack(gather(mid, where), gather(midm, where))
+        )
+
+    def strided_sums(where):
+        pconv[...] += dot_t(
+            stack(gather(grad, where), gather(gradm, where)), stack(gather(x1m, where), gather(x0, where))
+        )
+
+    def pieces_of(b, margin):
+        edges = [margin] + list(range(chunk, span - margin, chunk)) + [span - margin]
+        return [(b, t, e - t) for t, e in zip(edges, edges[1:])]
+
+    def first(b):
+        def start():
+            for fetch in fetches(b):
+                fetch.wait()
+            for t in range(0, span, chunk):
+                stage0(b, t, chunk)
+
+        return [start] + [functools.partial(stage1, [piece]) for piece in pieces_of(b, EDGE)]
+
+    def later(piece):
+        b, t, n = piece
+        skip = EDGE if t == 3 * EDGE else 0
+        return b, t + skip, n - skip
+
+    def second(b):
+        work = [functools.partial(stage2, [piece]) for piece in pieces_of(b, 2 * EDGE)]
+        for piece in pieces_of(b, 3 * EDGE):
+            work += [
+                functools.partial(stage3, [piece]),
+                functools.partial(dilated_sums, [piece]),
+                functools.partial(strided_sums, [later(piece)]),
+            ]
+        return work
+
+    def run(work):
+        for step in work:
+            step()
+
+    run(first(0))
+    pl.semaphore_wait(barrier, count - 1)
+    for side in range(2):
+        @pl.when(has[side])
         def _():
-            pl.semaphore_wait(barrier, count - 1)
-            for side in range(2):
-                @pl.when(has[side])
-                def _():
-                    for move in moves(side):
-                        move.start()
-
-        return carry
-
-    lax.fori_loop(0, clips, first, 0)
+            for move in moves(side):
+                move.start()
+    for b in range(clips):
+        work, ahead = second(b), first(b + 1) if b + 1 < clips else []
+        order = []
+        while work or ahead:
+            order += work[:2] + ahead[:1]
+            work, ahead = work[2:], ahead[1:]
+        run(order)
 
     for side in range(2):
         @pl.when(has[side])
@@ -261,71 +342,31 @@
             for move in moves(1 - side):
                 move.wait_recv()
 
-    sides = ((0, -EDGE), (1, span))
-
-    def outside(b, carry):
-        lows = [tall(masks(b, t, EDGE).astype(BF16), ch // 16) for _, t in sides]
-        for (side, t), low in zip(sides, lows):
-            here = slice(t + OFF, t + OFF + EDGE)
-            even = xh[side, b, :ch] * low
-            odd = xh[side, b, ch:]
-            x0[b, :, here] = even
-            x1[b, :, here] = odd
-            put(x0p, b, t + OFF - 1, even)
-            put(x1m, b, t + OFF + 1, odd)
-            bg[b, :, here] = ogh[side, b] * low
-        starts = (-EDGE, span - EDGE)
-        spots = [slice(t + OFF, t + OFF + 2 * EDGE) for t in starts]
-        both = lambda ref: beside(*[ref[b, :, spot] for spot in spots])
-        h = dot(wc[...], stack(both(x1m), both(x0), both(x1), both(x0p))) + wide(biases[0], 4)
-        value, s = gelu_parts(h)
-        for k, t in enumerate(starts):
-            cut = slice(2 * k * EDGE, 2 * (k + 1) * EDGE)
-            half[b, :, spots[k]] = h[:, cut]
-            slope[b, :, spots[k]] = s[:, cut]
-            low = tall(masks(b, t, 2 * EDGE).astype(BF16), ch // 16)
-            shifted((mid, midm, midp), b, t, DILATION, value[:, cut].astype(BF16) * low)
-        spots = [slice(t + OFF, t + OFF + EDGE) for _, t in sides]
-        d = dot(wd[...], stack(both(midm), both(mid), both(midp))) + wide(biases[1], 2)
-        _, s = gelu_parts(d)
-        low = (dot(wu[...], both(bg)) * s).astype(BF16)
-        for k, (side, t) in enumerate(sides):
-            shifted((pre, prem, prep), b, t, DILATION, low[:, k * EDGE : (k + 1) * EDGE])
-        return carry
-
-    lax.fori_loop(0, clips, outside, 0)
-
-    ones = jnp.ones((16, chunk), BF16)
-
-    def second(b, carry):
-        for t in range(0, span, chunk):
-            here = slice(t + OFF, t + OFF + chunk)
-            d = dot(wd[...], stack(midm[b, :, here], mid[b, :, here], midp[b, :, here]))
-            d = d + wide(biases[1], chunk // EDGE)
-            value, s = gelu_parts(d)
-            low = value.astype(BF16)
-            gated[b, :, t : t + chunk] = low
-            pg = dot(wu[...], bg[b, :, here]) * s
-            psum[1] += lane_groups(pg)
-            shifted((pre, prem, prep), b, t, DILATION, pg.astype(BF16))
-            pmix[:, : ch + 16] += dot_t(bg[b, :, here], stack(low, ones))
-        for t in range(0, span, chunk):
-            here = slice(t + OFF, t + OFF + chunk)
-            mask = tall(masks(b, t, chunk), ch // 16)
-            mid_grad = dot(wdt[...], stack(prep[b, :, here], pre[b, :, here], prem[b, :, here]))
-            g = (bg[b, :, here].astype(F32) + mid_grad * slope[b, :, here]) * mask
-            psum[0] += lane_groups(g)
-            shifted((grad, gradm, gradp), b, t, 1, g.astype(BF16))
-            pdil[...] += dot_t(
-                stack(pre[b, :, here], prem[b, :, here]), stack(mid[b, :, here], midm[b, :, here])
-            )
-        wide_here = slice(OFF, OFF + span + EDGE)
-        pconv[...] += dot_t(
-            stack(grad[b, :, wide_here], gradm[b, :, wide_here]), stack(x1m[b, :, wide_here], x0[b, :, wide_here])
-        )
-        return carry
-
-    lax.fori_loop(0, clips, second, 0)
+    def edge(width):
+        return [
+            (b, -EDGE if side == 0 else span - width, width + EDGE) for b in range(clips) for side in range(2)
+        ]
+
+    for b, t, n in edge(0):
+        side = 0 if t < 0 else 1
+        low = lows([(b, t, n)])
+        even = xh[side, b, :ch] * low
+        odd = xh[side, b, ch:]
+        x0[b, :, spot(t, n)] = even
+        x1[b, :, spot(t, n)] = odd
+        put(x0p, b, t + OFF - 1, even)
+        put(x1m, b, t + OFF + 1, odd)
+        bg[b, :, spot(t, n)] = ogh[side, b] * low
+    stage1(edge(EDGE))
+    stage2(edge(2 * EDGE))
+    low = stage3(edge(3 * EDGE))
+    dilated_sums(own(edge(3 * EDGE))[0])
+    strided_sums([(b, max(t, 0), 4 * EDGE) for b, t, _ in edge(3 * EDGE)])
+    for b, t, n, cut in cuts(edge(3 * EDGE)):
+        if t < 0:
+            put(gradm, b, t + OFF + 1, low[:, cut.start : cut.start + EDGE])
+        else:
+            put(gradp, b, span + OFF - 1, low[:, cut.stop - EDGE : cut.stop])
 
     at = 0
     flat = [
@@ -356,16 +397,6 @@
             ).start()
 
     def third(b, carry):
-        for k, (side, t) in enumerate(sides):
-            here = slice(t + OFF, t + OFF + EDGE)
-            mask = tall(masks(b, t, EDGE), ch // 16)
-            mid_grad = dot(wdt[...], stack(prep[b, :, here], pre[b, :, here], prem[b, :, here]))
-            g = (bg[b, :, here].astype(F32) + mid_grad * slope[b, :, here]) * mask
-            low = g.astype(BF16)
-            if side == 0:
-                put(gradm, b, t + OFF + 1, low)
-            else:
-                put(gradp, b, t + OFF - 1, low)
         for t in range(0, span, chunk):
             here = slice(t + OFF, t + OFF + chunk)
             there = slice(t, t + chunk)
@@ -440,8 +471,7 @@
         ],
         scratch_shapes=[
             pltpu.VMEM((ch, 4 * ch), BF16),
-            pltpu.VMEM((ch, 3 * ch), BF16),
-            pltpu.VMEM((ch, ch), BF16),
+            pltpu.VMEM((2 * ch, 4 * ch), BF16),
             pltpu.VMEM((ch, ch), BF16),
             pltpu.VMEM((ch, 3 * ch), BF16),
             pltpu.VMEM((2 * ch, 3 * ch), BF16),

time: 35.3 us -> 32.1 us (0.909)
  Pallas kernels: 34.5 us -> 31.3 us
    pallas_call x1, Pallas kernels: 31 us -> 27.9 us  [body(): layer_call(rows, parts, clips, span, pieces)]
where the time goes in v3:
time: 32.1 us; the launch traced here: 32 us
  Pallas kernels  31.3 us (98%)
  between operations  0.64 us (2%)
    pallas_call x1, Pallas kernels, body(): layer_call(rows, parts, clips, span, pieces)  27.9 us
    pallas_call x1, Pallas kernels, body(): hand_over_call(layer_out, clips_grad)  3.45 us

profile of v3, /device:TPU:0, one launch (start us, length us, event | category | flops | bytes accessed | tf_op | source)
XLA Modules:
  0.0 32.0 jit_solution(8580675302697692485)
XLA Ops:
  0.6 27.9 %layer.1 = (bf16[4,64,4096]{2,1,0:T(8,128)(2,1)S(1)}, bf16[4,128,4096]{2,1,0:T(8,128)(2,1)S(1)}, bf16[9,32,128]{2,1,0:T(8,128)(2,1)S(1)}) custom-call(s32[4]{0:T(128)} %counts.1, s32[4]{0:T(128)} %groups.1, bf16[4,128,4096]{2,1,0:T(8,128)(2,1)} %x_ref.1, bf16[4,64,4096]{2,1,0:T(8,128)(2,1)} %og_ref.1, bf16[64,4,64]{2,1,0:T(4,128)(2,1)} %bitcast.12, ...), custom_call_target="tpu_custom_call" | custom-call | tf_op jit(solution)/shard_map/layer/pallas_call | solution.py:551
  28.5 3.5 %hand_over.1 = (bf16[4,64,4096]{2,1,0:T(8,128)(2,1)}, bf16[4,128,4096]{2,1,0:T(8,128)(2,1)}, f32[64,4,64]{2,1,0:T(4,128)}, f32[1,64]{1,0:T(1,128)}, f32[3,64,64]...) custom-call(bf16[4,64,4096]{2,1,0:T(8,128)(2,1)S(1)} %get-tuple-element.19.out_in, ...), custom_call_target="tpu_custom_call" | custom-call | tf_op jit(solution)/shard_map/hand_over/pallas_call | solution.py:554

commit v4 on v3

--- a/solution.py
+++ b/solution.py
@@ -10,7 +10,10 @@
 DILATION = 27
 EDGE = 128
 OFF = 2 * EDGE
-CHUNK = 2048
+CHUNK = 4096
+SUB = 256
+SUMS = 1024
+RATIO = 2
 PIECE = 32
 MESH = pl.DeviceIdType.MESH
 F32 = jnp.float32
@@ -70,16 +73,16 @@
     rows,
     parts,
     owners,
-    counts,
-    groups,
+    counts_ref,
+    groups_ref,
     x_ref,
     og_ref,
-    cw,
-    dw,
-    mw,
-    cb,
-    db,
-    mb,
+    cw_ref,
+    dw_ref,
+    mw_ref,
+    cb_ref,
+    db_ref,
+    mb_ref,
     outs,
     dxs,
     total_ref,
@@ -114,6 +117,15 @@
     psum,
     parcel,
     slots,
+    counts,
+    groups,
+    cw,
+    dw,
+    mw,
+    cb,
+    db,
+    mb,
+    small_sem,
     in_sem,
     send,
     recv,
@@ -148,14 +160,30 @@
             pltpu.make_async_copy(og_ref.at[b], bg.at[b, :, inside], in_sem.at[b, 2]),
         ]
 
-    for b in range(clips):
-        for fetch in fetches(b):
-            fetch.start()
+    small = [
+        pltpu.make_async_copy(src, dst, small_sem.at[k])
+        for k, (src, dst) in enumerate(
+            (
+                (cw_ref, cw),
+                (dw_ref, dw),
+                (mw_ref, mw),
+                (cb_ref, cb),
+                (db_ref, db),
+                (mb_ref, mb),
+                (counts_ref, counts),
+                (groups_ref, groups),
+            )
+        )
+    ]
+    for fetch in small + fetches(0) + fetches(1):
+        fetch.start()
     xh[...] = jnp.zeros(xh.shape, BF16)
     ogh[...] = jnp.zeros(ogh.shape, BF16)
     barrier = pltpu.get_barrier_semaphore()
     others(lambda r, p: pl.semaphore_signal(barrier, inc=1, device_id=(r, p), device_id_type=MESH))
 
+    for fetch in small:
+        fetch.wait()
     flip = lambda w: w.astype(F32).T.astype(BF16)
     taps = [cw[:, k, :] for k in range(4)]
     zero = jnp.zeros((ch, ch), BF16)
@@ -235,15 +263,27 @@
         put(x1m, b, t + OFF + 1, x1[b, :, here])
         bg[b, :, here] = bg[b, :, here] * low
 
+    def tiles(where):
+        found = []
+        for b, t, n, cut in cuts(where):
+            at = t
+            while at < t + n:
+                stop = min([at + SUB, t + n] + [border for border in (0, span) if border > at])
+                found.append(((b, at, stop - at), slice(cut.start + at - t, cut.start + stop - t)))
+                at = stop
+        return found
+
     def stage1(where):
         taps = stack(gather(x1m, where), gather(x0, where), gather(x1, where), gather(x0p, where))
-        h = dot(wc[...], taps)
-        h = h + wide(biases[0], h.shape[1] // EDGE)
-        value, s = gelu_parts(h)
-        for b, t, n, cut in cuts(where):
-            half[b, :, spot(t, n)] = h[:, cut]
-            slope[b, :, spot(t, n)] = s[:, cut]
-        spread((mid, midm, midp), where, DILATION, value.astype(BF16) * lows(where))
+        product = dot(wc[...], taps)
+        yield
+        for (b, t, n), cut in tiles(where):
+            h = product[:, cut] + wide(biases[0], n // EDGE)
+            value, s = gelu_parts(h)
+            half[b, :, spot(t, n)] = h
+            slope[b, :, spot(t, n)] = s
+            spread((mid, midm, midp), [(b, t, n)], DILATION, value.astype(BF16) * lows([(b, t, n)]))
+            yield
 
     def own(where):
         kept = [(b, max(t, 0), min(t + n, span) - max(t, 0)) for b, t, n in where]
@@ -252,32 +292,50 @@
             for (b, t, n, cut), (_, kt, kn) in zip(cuts(where), kept)
         ]
 
+    def inside_of(t, n):
+        return 0 <= t and t + n <= span
+
     def stage2(where):
         taps = stack(gather(midm, where), gather(mid, where), gather(midp, where), gather(bg, where))
         both = dot(wd[...], taps)
-        d = both[:ch] + wide(biases[1], both.shape[1] // EDGE)
-        value, s = gelu_parts(d)
-        pg = both[ch:] * s
-        spread((pre, prem, prep), where, DILATION, pg.astype(BF16))
-        kept, inner = own(where)
-        low = value.astype(BF16)
-        for (b, t, n), cut in zip(kept, inner):
-            gated[b, :, t : t + n] = low[:, cut]
-            psum[1] += lane_groups(pg[:, cut])
-        low = beside(*[low[:, cut] for cut in inner])
-        ones = jnp.ones((16, low.shape[1]), BF16)
-        pmix[:, : ch + 16] += dot_t(gather(bg, kept), stack(low, ones))
-
-    def stage3(where, halo=False):
+        yield
+        lows_of, kept = [], []
+        for (b, t, n), cut in tiles(where):
+            d = both[:ch, cut] + wide(biases[1], n // EDGE)
+            value, s = gelu_parts(d)
+            pg = both[ch:, cut] * s
+            spread((pre, prem, prep), [(b, t, n)], DILATION, pg.astype(BF16))
+            if inside_of(t, n):
+                low = value.astype(BF16)
+                gated[b, :, t : t + n] = low
+                psum[1] += lane_groups(pg)
+                lows_of.append(low)
+                kept.append((b, t, n))
+            yield
+        low = beside(*lows_of)
+        pmix[:, : ch + 16] += dot_t(gather(bg, kept), stack(low, jnp.ones((16, low.shape[1]), BF16)))
+        yield
+
+    def stage3(where, halo=None):
         mid_grad = dot(wdt[...], stack(gather(prep, where), gather(pre, where), gather(prem, where)))
-        mask = beside(*[tall(masks(b, t, n), ch // 16) for b, t, n in where])
-        g = (gather(bg, where).astype(F32) + mid_grad * gather(slope, where)) * mask
-        low = g.astype(BF16)
-        kept, inner = own(where)
-        for (b, t, n), cut in zip(kept, inner):
-            psum[0] += lane_groups(g[:, cut])
-            spread((grad, gradm, gradp), [(b, t, n)], 1, low[:, cut])
-        return low
+        yield
+        for (b, t, n), cut in tiles(where):
+            mask = tall(masks(b, t, n), ch // 16)
+            here = spot(t, n)
+            g = (bg[b, :, here].astype(F32) + mid_grad[:, cut] * slope[b, :, here]) * mask
+            low = g.astype(BF16)
+            if inside_of(t, n):
+                psum[0] += lane_groups(g)
+                spread((grad, gradm, gradp), [(b, t, n)], 1, low)
+            elif halo is not None:
+                halo.append((b, t, low))
+            yield
+
+    def by_steps(sums, where):
+        for b, t, n in where:
+            for k in range(0, n, SUMS):
+                sums([(b, t + k, min(SUMS, n - k))])
+                yield
 
     def dilated_sums(where):
         pdil[...] += dot_t(
@@ -294,13 +352,11 @@
         return [(b, t, e - t) for t, e in zip(edges, edges[1:])]
 
     def first(b):
-        def start():
-            for fetch in fetches(b):
-                fetch.wait()
-            for t in range(0, span, chunk):
-                stage0(b, t, chunk)
-
-        return [start] + [functools.partial(stage1, [piece]) for piece in pieces_of(b, EDGE)]
+        for t in range(0, span, chunk):
+            stage0(b, t, chunk)
+            yield
+        for piece in pieces_of(b, EDGE):
+            yield from stage1([piece])
 
     def later(piece):
         b, t, n = piece
@@ -308,19 +364,59 @@
         return b, t + skip, n - skip
 
     def second(b):
-        work = [functools.partial(stage2, [piece]) for piece in pieces_of(b, 2 * EDGE)]
+        for piece in pieces_of(b, 2 * EDGE):
+            yield from stage2([piece])
         for piece in pieces_of(b, 3 * EDGE):
-            work += [
-                functools.partial(stage3, [piece]),
-                functools.partial(dilated_sums, [piece]),
-                functools.partial(strided_sums, [later(piece)]),
-            ]
-        return work
+            yield from stage3([piece])
+            yield from by_steps(dilated_sums, [piece])
+            yield from by_steps(strided_sums, [later(piece)])
+
+    def mix(main, side, ratio):
+        done = object()
+        while True:
+            ended = [next(main, done) is done for _ in range(ratio)]
+            if next(side, done) is done and ended[-1]:
+                return
 
     def run(work):
-        for step in work:
-            step()
-
+        for _ in work:
+            pass
+
+    def edge(width):
+        return [
+            (b, -EDGE if side == 0 else span - width, width + EDGE) for b in range(clips) for side in range(2)
+        ]
+
+    def outside():
+        for b, t, n in edge(0):
+            side = 0 if t < 0 else 1
+            low = lows([(b, t, n)])
+            even = xh[side, b, :ch] * low
+            odd = xh[side, b, ch:]
+            x0[b, :, spot(t, n)] = even
+            x1[b, :, spot(t, n)] = odd
+            put(x0p, b, t + OFF - 1, even)
+            put(x1m, b, t + OFF + 1, odd)
+            bg[b, :, spot(t, n)] = ogh[side, b] * low
+        yield
+        yield from stage1(edge(EDGE))
+        yield from stage2(edge(2 * EDGE))
+        halo = []
+        yield from stage3(edge(3 * EDGE), halo)
+        dilated_sums(own(edge(3 * EDGE))[0])
+        strided_sums([(b, max(t, 0), 4 * EDGE) for b, t, _ in edge(3 * EDGE)])
+        for b, t, low in halo:
+            if t < 0:
+                put(gradm, b, t + OFF + 1, low)
+            else:
+                put(gradp, b, t + OFF - 1, low)
+        yield
+
+    def arrive(b):
+        for fetch in fetches(b):
+            fetch.wait()
+
+    arrive(0)
     run(first(0))
     pl.semaphore_wait(barrier, count - 1)
     for side in range(2):
@@ -328,45 +424,19 @@
         def _():
             for move in moves(side):
                 move.start()
-    for b in range(clips):
-        work, ahead = second(b), first(b + 1) if b + 1 < clips else []
-        order = []
-        while work or ahead:
-            order += work[:2] + ahead[:1]
-            work, ahead = work[2:], ahead[1:]
-        run(order)
+    for b in range(clips - 1):
+        arrive(b + 1)
+        if b + 2 < clips:
+            for fetch in fetches(b + 2):
+                fetch.start()
+        mix(second(b), first(b + 1), RATIO)
 
     for side in range(2):
         @pl.when(has[side])
         def _():
             for move in moves(1 - side):
                 move.wait_recv()
-
-    def edge(width):
-        return [
-            (b, -EDGE if side == 0 else span - width, width + EDGE) for b in range(clips) for side in range(2)
-        ]
-
-    for b, t, n in edge(0):
-        side = 0 if t < 0 else 1
-        low = lows([(b, t, n)])
-        even = xh[side, b, :ch] * low
-        odd = xh[side, b, ch:]
-        x0[b, :, spot(t, n)] = even
-        x1[b, :, spot(t, n)] = odd
-        put(x0p, b, t + OFF - 1, even)
-        put(x1m, b, t + OFF + 1, odd)
-        bg[b, :, spot(t, n)] = ogh[side, b] * low
-    stage1(edge(EDGE))
-    stage2(edge(2 * EDGE))
-    low = stage3(edge(3 * EDGE))
-    dilated_sums(own(edge(3 * EDGE))[0])
-    strided_sums([(b, max(t, 0), 4 * EDGE) for b, t, _ in edge(3 * EDGE)])
-    for b, t, n, cut in cuts(edge(3 * EDGE)):
-        if t < 0:
-            put(gradm, b, t + OFF + 1, low[:, cut.start : cut.start + EDGE])
-        else:
-            put(gradp, b, span + OFF - 1, low[:, cut.stop - EDGE : cut.stop])
+    mix(second(clips - 1), outside(), RATIO)
 
     at = 0
     flat = [
@@ -410,32 +480,33 @@
 
     lax.fori_loop(0, clips, third, 0)
 
-    for piece, (r, p) in enumerate(owners):
-        @pl.when(me == r * parts + p)
-        def _():
-            pltpu.make_async_copy(slots, slots, recv1).wait()
-            total = parcel[piece].astype(F32)
-            for k in range(count - 1):
-                total = total + slots[k].astype(F32)
-            total_ref[piece] = total.astype(BF16)
-            others(
-                lambda tr, tp: pltpu.make_async_remote_copy(
-                    src_ref=total_ref.at[piece],
-                    dst_ref=total_ref.at[piece],
-                    send_sem=send2,
-                    recv_sem=recv2,
-                    device_id=(tr, tp),
-                    device_id_type=MESH,
-                ).start()
-            )
+    homes = [r * parts + p for r, p in owners]
+    owner = functools.reduce(jnp.logical_or, [me == home for home in homes])
+    mine = sum(jnp.where(me == home, piece, 0) for piece, home in enumerate(homes))
+
+    @pl.when(owner)
+    def _():
+        pltpu.make_async_copy(slots, slots, recv1).wait()
+        total = parcel[mine].astype(F32)
+        for k in range(count - 1):
+            total = total + slots[k].astype(F32)
+        total_ref[mine] = total.astype(BF16)
+        for k in range(1, count):
+            target = lax.rem(me + k, count)
+            pltpu.make_async_remote_copy(
+                src_ref=total_ref.at[mine],
+                dst_ref=total_ref.at[mine],
+                send_sem=send2,
+                recv_sem=recv2,
+                device_id=(target // parts, lax.rem(target, parts)),
+                device_id_type=MESH,
+            ).start()
 
     for side in range(2):
         @pl.when(has[side])
         def _():
             for move in moves(side):
                 move.wait_send()
-    owner = functools.reduce(jnp.logical_or, [me == r * parts + p for r, p in owners])
-
     @pl.when(owner)
     def _():
         rest = total_ref.at[pl.ds(0, pieces - 1)]
@@ -453,7 +524,6 @@
 def layer_call(rows, parts, clips, span, pieces):
     ch = 64
     lanes = span + 4 * EDGE
-    smem = pl.BlockSpec(memory_space=pltpu.SMEM)
     vmem = pl.BlockSpec(memory_space=pltpu.VMEM)
     hbm = pl.BlockSpec(memory_space=pl.ANY)
     low = pltpu.VMEM((clips, ch, lanes), BF16)
@@ -462,7 +532,7 @@
     return pl.pallas_call(
         functools.partial(layer, rows, parts, owner_list(rows, parts, pieces)),
         name="layer",
-        in_specs=[smem, smem, hbm, hbm] + [vmem] * 6,
+        in_specs=[hbm] * 10,
         out_specs=[vmem, vmem, vmem],
         out_shape=[
             pltpu.VMEM((clips, ch, span), BF16),
@@ -491,6 +561,15 @@
             pltpu.VMEM((2, ch, EDGE), F32),
             pltpu.VMEM((pieces, PIECE, 2 * ch), BF16),
             pltpu.VMEM((rows * parts - 1, PIECE, 2 * ch), BF16),
+            pltpu.SMEM((clips,), jnp.int32),
+            pltpu.SMEM((clips,), jnp.int32),
+            pltpu.VMEM((ch, 4, ch), BF16),
+            pltpu.VMEM((3, ch, ch), BF16),
+            pltpu.VMEM((ch, ch), BF16),
+            pltpu.VMEM((1, ch), F32),
+            pltpu.VMEM((1, ch), F32),
+            pltpu.VMEM((1, ch), F32),
+            dma((8,)),
             dma((clips, 3)),
             dma((2, 2)),
             dma((2, 2)),
@@ -503,7 +582,9 @@
     )
 
 
-def hand_over(out_in, clips_in, sums, out, clips, cg, cb, dg, db, mg, mb, sem):
+def hand_over(out_in, clips_in, sums, *refs):
+    out, clips = refs[:2]
+    finals, (cg, cb, dg, db, mg, mb), (sem, small_sem) = refs[2:8], refs[8:14], refs[14:]
     ch = 64
     moves = []
     for b in range(out.shape[0]):
@@ -524,6 +605,9 @@
     lines = at(4 * ch, 16)[:, :ch]
     for k, ref in enumerate((cb, db, mb)):
         ref[...] = lines[k : k + 1]
+    for k, (src, dst) in enumerate(zip((cg, cb, dg, db, mg, mb), finals)):
+        moves.append(pltpu.make_async_copy(src, dst, small_sem.at[k]))
+        moves[-1].start()
     for move in moves:
         move.wait()
 
@@ -537,10 +621,11 @@
     return pl.pallas_call(
         hand_over,
         name="hand_over",
-        in_specs=[vmem, vmem, vmem],
-        out_specs=[hbm, hbm] + [vmem] * 6,
+        in_specs=[vmem] * 3,
+        out_specs=[hbm] * 8,
         out_shape=[like(out), like(clips)] + [jax.ShapeDtypeStruct(s, F32) for s in shapes],
-        scratch_shapes=[pltpu.SemaphoreType.DMA((out.shape[0], 2))],
+        scratch_shapes=[pltpu.VMEM(s, F32) for s in shapes]
+        + [pltpu.SemaphoreType.DMA((out.shape[0], 2)), pltpu.SemaphoreType.DMA((6,))],
         compiler_params=pltpu.CompilerParams(vmem_limit_bytes=8 << 20),
     )
 

time: 32.1 us -> 29.7 us (0.925)
  Pallas kernels: 31.3 us -> 28.9 us
    pallas_call x1, Pallas kernels: 27.9 us -> 26.1 us  [body(): layer_call(rows, parts, clips, span, pieces)]
    pallas_call x1, Pallas kernels: 3.45 us -> 2.84 us  [body(): hand_over_call(layer_out, clips_grad)]
where the time goes in v4:
time: 29.7 us; the launch traced here: 29.6 us
  Pallas kernels  28.9 us (97%)
  between operations  0.64 us (2%)
    pallas_call x1, Pallas kernels, body(): layer_call(rows, parts, clips, span, pieces)  26.1 us
    pallas_call x1, Pallas kernels, body(): hand_over_call(layer_out, clips_grad)  2.84 us

profile of v4, /device:TPU:0, one launch (start us, length us, event | category | flops | bytes accessed | tf_op | source)
XLA Modules:
  0.0 29.6 jit_solution(10843992009664578173)
XLA Ops:
  0.6 26.1 %layer.1 = (bf16[4,64,4096]{2,1,0:T(8,128)(2,1)S(1)}, bf16[4,128,4096]{2,1,0:T(8,128)(2,1)S(1)}, bf16[9,32,128]{2,1,0:T(8,128)(2,1)S(1)}) custom-call(s32[4]{0:T(128)} %counts_ref.1, s32[4]{0:T(128)} %groups_ref.1, bf16[4,128,4096]{2,1,0:T(8,128)(2,1)} %x_ref.1, bf16[4,64,4096]{2,1,0:T(8,128)(2,1)} %og_ref.1, bf16[64,4,64]{2,1,0:T(4,128)(2,1)} %bitcast.12, ...), custom_call_target="tpu_custom_call" | custom-call | tf_op jit(solution)/shard_map/layer/pallas_call | solution.py:636
  26.7 2.8 %hand_over.1 = (bf16[4,64,4096]{2,1,0:T(8,128)(2,1)}, bf16[4,128,4096]{2,1,0:T(8,128)(2,1)}, f32[64,4,64]{2,1,0:T(4,128)}, f32[1,64]{1,0:T(1,128)}, f32[3,64,64]...) custom-call(bf16[4,64,4096]{2,1,0:T(8,128)(2,1)S(1)} %get-tuple-element.19.out_in, ...), custom_call_target="tpu_custom_call" | custom-call | tf_op jit(solution)/shard_map/hand_over/pallas_call | solution.py:639

commit v5 on v4

--- a/solution.py
+++ b/solution.py
@@ -14,7 +14,8 @@
 SUB = 256
 SUMS = 1024
 RATIO = 2
-PIECE = 32
+ROWS = 16
+OWNERS = 8
 MESH = pl.DeviceIdType.MESH
 F32 = jnp.float32
 BF16 = jnp.bfloat16
@@ -61,12 +62,14 @@
     return total
 
 
-def owner_list(rows, parts, pieces):
+def owner_list(rows, parts, blocks):
     half = parts // 2
     order = sorted(range(half), key=lambda q: abs(2 * q - half + 1))
-    spots = [(r, 2 * q + 1) for q in order for r in range(rows)]
-    spots += [(r, 2 * q) for q in order for r in range(rows)]
-    return spots[:pieces]
+    spots = [r * parts + 2 * q + 1 for q in order for r in range(rows)][:OWNERS]
+    share = blocks // len(spots)
+    return [
+        (home, k * share, share if k + 1 < len(spots) else blocks - k * share) for k, home in enumerate(spots)
+    ]
 
 
 def layer(
@@ -115,6 +118,8 @@
     pdil,
     pmix,
     psum,
+    mask_high,
+    mask_low,
     parcel,
     slots,
     counts,
@@ -137,7 +142,6 @@
     ch = 64
     clips, _, span = og_ref.shape
     chunk = min(CHUNK, span)
-    pieces = len(owners)
     count = rows * parts
     row, place = lax.axis_index("batch"), lax.axis_index("tm")
     me = row * parts + place
@@ -175,7 +179,7 @@
             )
         )
     ]
-    for fetch in small + fetches(0) + fetches(1):
+    for fetch in fetches(0)[:2] + small + fetches(0)[2:]:
         fetch.start()
     xh[...] = jnp.zeros(xh.shape, BF16)
     ogh[...] = jnp.zeros(ogh.shape, BF16)
@@ -202,15 +206,24 @@
     for k, line in enumerate((cb, db, mb)):
         biases[k] = jnp.broadcast_to(line[...] * 0.5, (EDGE, ch)).T
 
+    lanes = span + 4 * EDGE
+    frame = base - OFF + lax.broadcasted_iota(jnp.int32, (16, lanes), 1)
+    for b in range(clips):
+        valid = jnp.minimum(lax.shift_right_logical(counts[b], groups[b]), span * parts)
+        mask = jnp.where((frame >= 0) & (frame < valid), 1.0, 0.0)
+        mask_high[b] = mask[:8]
+        mask_low[b] = mask.astype(BF16)
+
     for ref, at in ((gradm, OFF), (gradm, OFF + span), (grad, OFF + span)):
         ref[:, :, at : at + EDGE] = jnp.zeros((clips, ch, EDGE), BF16)
     for ref in (pconv, pdil, pmix, psum):
         ref[...] = jnp.zeros(ref.shape, F32)
 
-    def masks(b, t, n, high=1.0):
-        valid = jnp.minimum(lax.shift_right_logical(counts[b], groups[b]), span * parts)
-        frame = base + t + lax.broadcasted_iota(jnp.int32, (16, n), 1)
-        return jnp.where((frame >= 0) & (frame < valid), high, 0.0)
+    def masks(b, t, n):
+        return mask_high[b, :, t + OFF : t + OFF + n]
+
+    def low_masks(b, t, n):
+        return mask_low[b, :, t + OFF : t + OFF + n]
 
     def put(ref, b, start, value):
         ref[b, :, start : start + value.shape[1]] = value
@@ -252,7 +265,7 @@
             put(after, b, t + OFF - step, low[:, cut])
 
     def lows(where):
-        return beside(*[tall(masks(b, t, n).astype(BF16), ch // 16) for b, t, n in where])
+        return beside(*[tall(low_masks(b, t, n), ch // 16) for b, t, n in where])
 
     def stage0(b, t, n):
         here = spot(t, n)
@@ -261,7 +274,6 @@
         x0[b, :, here] = even
         put(x0p, b, t + OFF - 1, even)
         put(x1m, b, t + OFF + 1, x1[b, :, here])
-        bg[b, :, here] = bg[b, :, here] * low
 
     def tiles(where):
         found = []
@@ -320,13 +332,14 @@
         mid_grad = dot(wdt[...], stack(gather(prep, where), gather(pre, where), gather(prem, where)))
         yield
         for (b, t, n), cut in tiles(where):
-            mask = tall(masks(b, t, n), ch // 16)
+            mask = tall(masks(b, t, n), ch // 8)
             here = spot(t, n)
             g = (bg[b, :, here].astype(F32) + mid_grad[:, cut] * slope[b, :, here]) * mask
             low = g.astype(BF16)
             if inside_of(t, n):
                 psum[0] += lane_groups(g)
-                spread((grad, gradm, gradp), [(b, t, n)], 1, low)
+                grad[b, :, spot(t, n)] = low
+                put(gradm, b, t + OFF + 1, low)
             elif halo is not None:
                 halo.append((b, t, low))
             yield
@@ -364,6 +377,9 @@
         return b, t + skip, n - skip
 
     def second(b):
+        for t in range(0, span, chunk):
+            bg[b, :, spot(t, chunk)] = bg[b, :, spot(t, chunk)] * lows([(b, t, chunk)])
+            yield
         for piece in pieces_of(b, 2 * EDGE):
             yield from stage2([piece])
         for piece in pieces_of(b, 3 * EDGE):
@@ -409,27 +425,32 @@
             if t < 0:
                 put(gradm, b, t + OFF + 1, low)
             else:
-                put(gradp, b, t + OFF - 1, low)
+                grad[b, :, spot(t, EDGE)] = low
         yield
 
     def arrive(b):
         for fetch in fetches(b):
             fetch.wait()
 
-    arrive(0)
+    for fetch in fetches(0)[:2]:
+        fetch.wait()
+    for fetch in fetches(1):
+        fetch.start()
     run(first(0))
-    pl.semaphore_wait(barrier, count - 1)
-    for side in range(2):
-        @pl.when(has[side])
-        def _():
-            for move in moves(side):
-                move.start()
+    fetches(0)[2].wait()
     for b in range(clips - 1):
         arrive(b + 1)
         if b + 2 < clips:
             for fetch in fetches(b + 2):
                 fetch.start()
         mix(second(b), first(b + 1), RATIO)
+        if b == 0:
+            pl.semaphore_wait(barrier, count - 1)
+            for side in range(2):
+                @pl.when(has[side])
+                def _():
+                    for move in moves(side):
+                        move.start()
 
     for side in range(2):
         @pl.when(has[side])
@@ -438,31 +459,25 @@
                 move.wait_recv()
     mix(second(clips - 1), outside(), RATIO)
 
-    at = 0
-    flat = [
-        pconv[...],
-        pdil[:ch, :],
-        beside(pdil[ch:, :ch], pmix[:, :ch]),
-    ]
+    flat = [pconv[...], pdil[:ch, :], beside(pdil[ch:, :ch], pmix[:, :ch])]
     lines = [jnp.sum(psum[k].T, axis=0, keepdims=True) for k in range(2)]
     lines.append(pmix[:, ch:].T[:1, :])
-    lines = stack(*lines, jnp.zeros((PIECE - 3, ch), F32))
+    lines = stack(*lines, jnp.zeros((ROWS - 3, ch), F32))
     flat.append(beside(lines, jnp.zeros_like(lines)))
+    at = 0
     for block in flat:
-        for start in range(0, block.shape[0], PIECE):
-            parcel[at] = block[start : start + PIECE, :].astype(BF16)
+        for start in range(0, block.shape[0], ROWS):
+            parcel[at] = block[start : start + ROWS, :].astype(BF16)
             at += 1
-    for piece, (r, p) in enumerate(owners):
-        home = r * parts + p
-
+    for home, start, n in owners:
         @pl.when(me != home)
         def _():
             pltpu.make_async_remote_copy(
-                src_ref=parcel.at[piece],
-                dst_ref=slots.at[lax.rem(me - home + count, count) - 1],
+                src_ref=parcel.at[pl.ds(start, n)],
+                dst_ref=slots.at[lax.rem(me - home + count, count) - 1, pl.ds(0, n)],
                 send_sem=send1,
                 recv_sem=recv1,
-                device_id=(r, p),
+                device_id=(home // parts, home % parts),
                 device_id_type=MESH,
             ).start()
 
@@ -470,50 +485,63 @@
         for t in range(0, span, chunk):
             here = slice(t + OFF, t + OFF + chunk)
             there = slice(t, t + chunk)
-            mask = masks(b, t, chunk, 2.0).astype(BF16)
+            low = low_masks(b, t, chunk)
             total = half[b, :, here] + dot(wm[...], gated[b, :, there]) + wide(biases[2], chunk // EDGE)
-            outs[b, :, there] = total.astype(BF16) * tall(mask, ch // 16)
-            low = masks(b, t, chunk).astype(BF16)
+            outs[b, :, there] = total.astype(BF16) * tall(low + low, ch // 16)
+            put(gradp, b, t + OFF - 1, grad[b, :, slice(t + OFF, t + OFF + chunk + EDGE)])
             dx = dot(wct[...], stack(gradm[b, :, here], grad[b, :, here], gradp[b, :, here]))
             dxs[b, :, there] = dx.astype(BF16) * tall(low, 2 * ch // 16)
         return carry
 
     lax.fori_loop(0, clips, third, 0)
 
-    homes = [r * parts + p for r, p in owners]
-    owner = functools.reduce(jnp.logical_or, [me == home for home in homes])
-    mine = sum(jnp.where(me == home, piece, 0) for piece, home in enumerate(homes))
-
-    @pl.when(owner)
-    def _():
-        pltpu.make_async_copy(slots, slots, recv1).wait()
-        total = parcel[mine].astype(F32)
-        for k in range(count - 1):
-            total = total + slots[k].astype(F32)
-        total_ref[mine] = total.astype(BF16)
-        for k in range(1, count):
-            target = lax.rem(me + k, count)
-            pltpu.make_async_remote_copy(
-                src_ref=total_ref.at[mine],
-                dst_ref=total_ref.at[mine],
-                send_sem=send2,
-                recv_sem=recv2,
-                device_id=(target // parts, lax.rem(target, parts)),
-                device_id_type=MESH,
-            ).start()
+    sizes = sorted({n for _, _, n in owners})
+    blocks = parcel.shape[0]
+    groups_of = [
+        (n, [(home, start) for home, start, m in owners if m == n]) for n in sizes
+    ]
+
+    def is_one(homes):
+        return functools.reduce(jnp.logical_or, [me == home for home, _ in homes])
+
+    for n, homes in groups_of:
+        @pl.when(is_one(homes))
+        def _():
+            start = sum(jnp.where(me == home, first_block, 0) for home, first_block in homes)
+            mine = pl.ds(start, n)
+            came = slots.at[:, pl.ds(0, n)]
+            pltpu.make_async_copy(came, came, recv1).wait()
+            total = parcel[mine].astype(F32)
+            for k in range(count - 1):
+                total = total + slots[k, :n].astype(F32)
+            total_ref[mine] = total.astype(BF16)
+            for k in range(1, count):
+                target = lax.rem(me + k, count)
+                pltpu.make_async_remote_copy(
+                    src_ref=total_ref.at[mine],
+                    dst_ref=total_ref.at[mine],
+                    send_sem=send2,
+                    recv_sem=recv2,
+                    device_id=(target // parts, lax.rem(target, parts)),
+                    device_id_type=MESH,
+                ).start()
 
     for side in range(2):
         @pl.when(has[side])
         def _():
             for move in moves(side):
                 move.wait_send()
-    @pl.when(owner)
-    def _():
-        rest = total_ref.at[pl.ds(0, pieces - 1)]
-        pltpu.make_async_copy(rest, rest, recv2).wait()
-        sent = parcel.at[pl.ds(0, pieces - 1)]
-        pltpu.make_async_copy(sent, sent, send1).wait()
-        pltpu.make_async_copy(slots, slots, send2).wait()
+    owner = is_one([(home, start) for home, start, _ in owners])
+    for n, homes in groups_of:
+        @pl.when(is_one(homes))
+        def _():
+            rest = total_ref.at[pl.ds(0, blocks - n)]
+            pltpu.make_async_copy(rest, rest, recv2).wait()
+            for _ in range(1, count):
+                one = total_ref.at[pl.ds(0, n)]
+                pltpu.make_async_copy(one, one, send2).wait()
+            sent = parcel.at[pl.ds(0, blocks - n)]
+            pltpu.make_async_copy(sent, sent, send1).wait()
 
     @pl.when(jnp.logical_not(owner))
     def _():
@@ -521,7 +549,7 @@
         pltpu.make_async_copy(parcel, parcel, send1).wait()
 
 
-def layer_call(rows, parts, clips, span, pieces):
+def layer_call(rows, parts, clips, span, blocks):
     ch = 64
     lanes = span + 4 * EDGE
     vmem = pl.BlockSpec(memory_space=pltpu.VMEM)
@@ -529,15 +557,16 @@
     low = pltpu.VMEM((clips, ch, lanes), BF16)
     high = pltpu.VMEM((clips, ch, lanes), F32)
     dma = pltpu.SemaphoreType.DMA
+    widest = max(n for _, _, n in owner_list(rows, parts, blocks))
     return pl.pallas_call(
-        functools.partial(layer, rows, parts, owner_list(rows, parts, pieces)),
+        functools.partial(layer, rows, parts, owner_list(rows, parts, blocks)),
         name="layer",
         in_specs=[hbm] * 10,
         out_specs=[vmem, vmem, vmem],
         out_shape=[
             pltpu.VMEM((clips, ch, span), BF16),
             pltpu.VMEM((clips, 2 * ch, span), BF16),
-            pltpu.VMEM((pieces, PIECE, 2 * ch), BF16),
+            pltpu.VMEM((blocks, ROWS, 2 * ch), BF16),
         ],
         scratch_shapes=[
             pltpu.VMEM((ch, 4 * ch), BF16),
@@ -559,8 +588,10 @@
             pltpu.VMEM((2 * ch, 2 * ch), F32),
             pltpu.VMEM((ch, 2 * ch), F32),
             pltpu.VMEM((2, ch, EDGE), F32),
-            pltpu.VMEM((pieces, PIECE, 2 * ch), BF16),
-            pltpu.VMEM((rows * parts - 1, PIECE, 2 * ch), BF16),
+            pltpu.VMEM((clips, 8, lanes), F32),
+            pltpu.VMEM((clips, 16, lanes), BF16),
+            pltpu.VMEM((blocks, ROWS, 2 * ch), BF16),
+            pltpu.VMEM((rows * parts - 1, widest, ROWS, 2 * ch), BF16),
             pltpu.SMEM((clips,), jnp.int32),
             pltpu.SMEM((clips,), jnp.int32),
             pltpu.VMEM((ch, 4, ch), BF16),
@@ -632,12 +663,12 @@
 
 def body(rows, parts, clips_in, cw, cb, dw, db, mw, mb, counts, groups, out_grad):
     clips, ch, span = out_grad.shape
-    pieces = -(-(4 * ch + 16) // PIECE)
-    layer_out, clips_grad, sums = layer_call(rows, parts, clips, span, pieces)(
+    blocks = (4 * ch + ROWS) // ROWS
+    layer_out, clips_grad, sums = layer_call(rows, parts, clips, span, blocks)(
         counts, groups, clips_in, out_grad, cw.transpose(0, 2, 1), dw.transpose(2, 0, 1), mw, cb[None], db[None], mb[None]
     )
     layer_out, clips_grad, cg, cbg, dg, dbg, mg, mbg = hand_over_call(layer_out, clips_grad)(
-        layer_out, clips_grad, sums.reshape(pieces * PIECE, 2 * ch)
+        layer_out, clips_grad, sums.reshape(blocks * ROWS, 2 * ch)
     )
     return (layer_out, clips_grad, cg.transpose(0, 2, 1), cbg[0], dg.transpose(1, 2, 0), dbg[0], mg, mbg[0])
 

time: 29.7 us -> 28.7 us (0.966)
  Pallas kernels: 28.9 us -> 27.9 us
    pallas_call x1, Pallas kernels: 26.1 us -> 25.1 us  [body(): layer_call(rows, parts, clips, span, blocks)]
where the time goes in v5:
time: 28.7 us; the launch traced here: 28.6 us
  Pallas kernels  27.9 us (97%)
  between operations  0.64 us (2%)
    pallas_call x1, Pallas kernels, body(): layer_call(rows, parts, clips, span, blocks)  25.1 us
    pallas_call x1, Pallas kernels, body(): hand_over_call(layer_out, clips_grad)  2.84 us

profile of v5, /device:TPU:0, one launch (start us, length us, event | category | flops | bytes accessed | tf_op | source)
XLA Modules:
  0.0 28.6 jit_solution(2871738515102359192)
XLA Ops:
  0.6 25.1 %layer.1 = (bf16[4,64,4096]{2,1,0:T(8,128)(2,1)S(1)}, bf16[4,128,4096]{2,1,0:T(8,128)(2,1)S(1)}, bf16[17,16,128]{2,1,0:T(8,128)(2,1)S(1)}) custom-call(s32[4]{0:T(128)} %counts_ref.1, s32[4]{0:T(128)} %groups_ref.1, bf16[4,128,4096]{2,1,0:T(8,128)(2,1)} %x_ref.1, bf16[4,64,4096]{2,1,0:T(8,128)(2,1)} %og_ref.1, bf16[64,4,64]{2,1,0:T(4,128)(2,1)} %bitcast.12, ...), custom_call_target="tpu_custom_call" | custom-call | tf_op jit(solution)/shard_map/layer/pallas_call | solution.py:667
  25.7 2.8 %hand_over.1 = (bf16[4,64,4096]{2,1,0:T(8,128)(2,1)}, bf16[4,128,4096]{2,1,0:T(8,128)(2,1)}, f32[64,4,64]{2,1,0:T(4,128)}, f32[1,64]{1,0:T(1,128)}, f32[3,64,64]...) custom-call(bf16[4,64,4096]{2,1,0:T(8,128)(2,1)S(1)} %get-tuple-element.19.out_in, ...), custom_call_target="tpu_custom_call" | custom-call | tf_op jit(solution)/shard_map/hand_over/pallas_call | solution.py:670

commit v6 on v5

--- a/solution.py
+++ b/solution.py
@@ -417,15 +417,9 @@
         yield
         yield from stage1(edge(EDGE))
         yield from stage2(edge(2 * EDGE))
-        halo = []
-        yield from stage3(edge(3 * EDGE), halo)
+        yield from stage3(own(edge(3 * EDGE))[0])
         dilated_sums(own(edge(3 * EDGE))[0])
         strided_sums([(b, max(t, 0), 4 * EDGE) for b, t, _ in edge(3 * EDGE)])
-        for b, t, low in halo:
-            if t < 0:
-                put(gradm, b, t + OFF + 1, low)
-            else:
-                grad[b, :, spot(t, EDGE)] = low
         yield
 
     def arrive(b):
@@ -438,19 +432,21 @@
         fetch.start()
     run(first(0))
     fetches(0)[2].wait()
-    for b in range(clips - 1):
-        arrive(b + 1)
-        if b + 2 < clips:
-            for fetch in fetches(b + 2):
-                fetch.start()
+    arrive(1)
+    for b in range(2, clips):
+        for fetch in fetches(b):
+            fetch.start()
+    mix(second(0), first(1), RATIO)
+    pl.semaphore_wait(barrier, count - 1)
+    for side in range(2):
+        @pl.when(has[side])
+        def _():
+            for move in moves(side):
+                move.start()
+    for b in range(2, clips):
+        arrive(b)
+    for b in range(1, clips - 1):
         mix(second(b), first(b + 1), RATIO)
-        if b == 0:
-            pl.semaphore_wait(barrier, count - 1)
-            for side in range(2):
-                @pl.when(has[side])
-                def _():
-                    for move in moves(side):
-                        move.start()
 
     for side in range(2):
         @pl.when(has[side])
@@ -480,6 +476,14 @@
                 device_id=(home // parts, home % parts),
                 device_id_type=MESH,
             ).start()
+
+    halo = []
+    run(stage3([(b, t, EDGE) for b in range(clips) for t in (-EDGE, span)], halo))
+    for b, t, low in halo:
+        if t < 0:
+            put(gradm, b, t + OFF + 1, low)
+        else:
+            grad[b, :, spot(t, EDGE)] = low
 
     def third(b, carry):
         for t in range(0, span, chunk):

time: 28.7 us -> 28.5 us (level)
  no operation moved by 1% of the time
where the time goes in v6:
time: 28.5 us; the launch traced here: 28.3 us
  Pallas kernels  27.7 us (97%)
  between operations  0.64 us (2%)
    pallas_call x1, Pallas kernels, body(): layer_call(rows, parts, clips, span, blocks)  24.9 us
    pallas_call x1, Pallas kernels, body(): hand_over_call(layer_out, clips_grad)  2.84 us

profile of v6, /device:TPU:0, one launch (start us, length us, event | category | flops | bytes accessed | tf_op | source)
XLA Modules:
  0.0 28.3 jit_solution(9724457585494827862)
XLA Ops:
  0.6 24.9 %layer.1 = (bf16[4,64,4096]{2,1,0:T(8,128)(2,1)S(1)}, bf16[4,128,4096]{2,1,0:T(8,128)(2,1)S(1)}, bf16[17,16,128]{2,1,0:T(8,128)(2,1)S(1)}) custom-call(s32[4]{0:T(128)} %counts_ref.1, s32[4]{0:T(128)} %groups_ref.1, bf16[4,128,4096]{2,1,0:T(8,128)(2,1)} %x_ref.1, bf16[4,64,4096]{2,1,0:T(8,128)(2,1)} %og_ref.1, bf16[64,4,64]{2,1,0:T(4,128)(2,1)} %bitcast.12, ...), custom_call_target="tpu_custom_call" | custom-call | tf_op jit(solution)/shard_map/layer/pallas_call | solution.py:671
  25.5 2.8 %hand_over.1 = (bf16[4,64,4096]{2,1,0:T(8,128)(2,1)}, bf16[4,128,4096]{2,1,0:T(8,128)(2,1)}, f32[64,4,64]{2,1,0:T(4,128)}, f32[1,64]{1,0:T(1,128)}, f32[3,64,64]...) custom-call(bf16[4,64,4096]{2,1,0:T(8,128)(2,1)S(1)} %get-tuple-element.19.out_in, ...), custom_call_target="tpu_custom_call" | custom-call | tf_op jit(solution)/shard_map/hand_over/pallas_call | solution.py:674

commit v7 on v6

--- a/solution.py
+++ b/solution.py
@@ -112,6 +112,8 @@
     grad,
     gradm,
     gradp,
+    x_edge,
+    og_edge,
     xh,
     ogh,
     pconv,
@@ -232,18 +234,29 @@
     other = (place - 1, place + 1)
 
     def moves(side):
-        cut = pl.ds(0, EDGE) if side == 0 else pl.ds(span - EDGE, EDGE)
         return [
             pltpu.make_async_remote_copy(
-                src_ref=src.at[:, :, cut],
+                src_ref=src.at[side],
                 dst_ref=dst.at[1 - side],
                 send_sem=send.at[side, k],
                 recv_sem=recv.at[1 - side, k],
                 device_id=(row, other[side]),
                 device_id_type=MESH,
             )
-            for k, (src, dst) in enumerate(((x_ref, xh), (og_ref, ogh)))
+            for k, (src, dst) in enumerate(((x_edge, xh), (og_edge, ogh)))
         ]
+
+    near = EDGE // 2
+
+    def swap(pair):
+        return beside(pair[:, near:], pair[:, :near])
+
+    def pack_edges():
+        for side, at in ((0, OFF), (1, OFF + span - near)):
+            for b in range(clips):
+                x_edge[side, b] = beside(x0[b, :, at : at + near], x1[b, :, at : at + near])
+            for b in range(0, clips, 2):
+                og_edge[side, b // 2] = beside(bg[b, :, at : at + near], bg[b + 1, :, at : at + near])
 
     def spot(t, n):
         return slice(t + OFF, t + OFF + n)
@@ -407,13 +420,15 @@
         for b, t, n in edge(0):
             side = 0 if t < 0 else 1
             low = lows([(b, t, n)])
-            even = xh[side, b, :ch] * low
-            odd = xh[side, b, ch:]
+            pair = xh[side, b]
+            even = (swap(pair) if side == 0 else pair) * low
+            odd = pair if side == 0 else swap(pair)
             x0[b, :, spot(t, n)] = even
             x1[b, :, spot(t, n)] = odd
             put(x0p, b, t + OFF - 1, even)
             put(x1m, b, t + OFF + 1, odd)
-            bg[b, :, spot(t, n)] = ogh[side, b] * low
+            pair = ogh[side, b // 2]
+            bg[b, :, spot(t, n)] = (pair if side != b % 2 else swap(pair)) * low
         yield
         yield from stage1(edge(EDGE))
         yield from stage2(edge(2 * EDGE))
@@ -437,14 +452,15 @@
         for fetch in fetches(b):
             fetch.start()
     mix(second(0), first(1), RATIO)
+    for b in range(2, clips):
+        arrive(b)
+    pack_edges()
     pl.semaphore_wait(barrier, count - 1)
     for side in range(2):
         @pl.when(has[side])
         def _():
             for move in moves(side):
                 move.start()
-    for b in range(2, clips):
-        arrive(b)
     for b in range(1, clips - 1):
         mix(second(b), first(b + 1), RATIO)
 
@@ -586,8 +602,10 @@
         + [pltpu.VMEM((clips, ch, span), BF16)]
         + [low] * 6
         + [
-            pltpu.VMEM((2, clips, 2 * ch, EDGE), BF16),
             pltpu.VMEM((2, clips, ch, EDGE), BF16),
+            pltpu.VMEM((2, clips // 2, ch, EDGE), BF16),
+            pltpu.VMEM((2, clips, ch, EDGE), BF16),
+            pltpu.VMEM((2, clips // 2, ch, EDGE), BF16),
             pltpu.VMEM((2 * ch, 2 * ch), F32),
             pltpu.VMEM((2 * ch, 2 * ch), F32),
             pltpu.VMEM((ch, 2 * ch), F32),

time: 28.5 us -> 28.7 us (level)
  no operation moved by 1% of the time
where the time goes in v7:
time: 28.7 us; the launch traced here: 28.5 us
  Pallas kernels  27.9 us (97%)
  between operations  0.64 us (2%)
    pallas_call x1, Pallas kernels, body(): layer_call(rows, parts, clips, span, blocks)  25 us
    pallas_call x1, Pallas kernels, body(): hand_over_call(layer_out, clips_grad)  2.84 us

profile of v7, /device:TPU:0, one launch (start us, length us, event | category | flops | bytes accessed | tf_op | source)
XLA Modules:
  0.0 28.5 jit_solution(9890608880675861079)
XLA Ops:
  0.6 25.0 %layer.1 = (bf16[4,64,4096]{2,1,0:T(8,128)(2,1)S(1)}, bf16[4,128,4096]{2,1,0:T(8,128)(2,1)S(1)}, bf16[17,16,128]{2,1,0:T(8,128)(2,1)S(1)}) custom-call(s32[4]{0:T(128)} %counts_ref.1, s32[4]{0:T(128)} %groups_ref.1, bf16[4,128,4096]{2,1,0:T(8,128)(2,1)} %x_ref.1, bf16[4,64,4096]{2,1,0:T(8,128)(2,1)} %og_ref.1, bf16[64,4,64]{2,1,0:T(4,128)(2,1)} %bitcast.12, ...), custom_call_target="tpu_custom_call" | custom-call | tf_op jit(solution)/shard_map/layer/pallas_call | solution.py:689
  25.7 2.8 %hand_over.1 = (bf16[4,64,4096]{2,1,0:T(8,128)(2,1)}, bf16[4,128,4096]{2,1,0:T(8,128)(2,1)}, f32[64,4,64]{2,1,0:T(4,128)}, f32[1,64]{1,0:T(1,128)}, f32[3,64,64]...) custom-call(bf16[4,64,4096]{2,1,0:T(8,128)(2,1)S(1)} %get-tuple-element.19.out_in, ...), custom_call_target="tpu_custom_call" | custom-call | tf_op jit(solution)/shard_map/hand_over/pallas_call | solution.py:692
